TPU v7x, 768 devices: a whole 4x8x12 slice. The times are simulated.
768 devices in a mesh: east: 96 (over z, y), north: 4 (over x), layer: 2 (over core).
Axes of the slice: x: 4, y: 8, z: 12, core: 2. Of those that a mesh axis runs over, the one named last changes fastest.
Arguments:
- recharge: float32 [8, 3072, 1024], P('layer', 'east', 'north'), may hold values from -16 to 16
- conductivity: float32 [8, 3072, 1024], P('layer', 'east', 'north'), may hold values from 0.1 to 10
- storage: float32 [8, 3072, 1024], P('layer', 'east', 'north'), may hold values from 0.1 to 1
Outputs:
- pressure: float32 [8, 3072, 1024], P('layer', 'east', 'north')
- residual: float32 [8, 3072, 1024], P('layer', 'east', 'north')
All inputs are finite; a program needn't handle non-finite values.
Results may differ from a plain program's by a relative error of at most 0.039.
Values sent between devices are 32-bit elements; how exact they have to be, the bound alone decides.
No kernel may reach another device: no remote copies, remote signals or barrier semaphores. Data moves between devices by JAX's collectives and lax.ppermute only.
A program may use at most 32 MiB of HBM per device.

v0:
```python
import jax
import jax.numpy as jnp
from jax import lax
from jax.sharding import PartitionSpec as P

ITERS = 2


def padded_2(block, sides, width):
    for axis, dim in sides:
        count = lax.axis_size(axis)
        forward = [(i, i + 1) for i in range(count - 1)]
        backward = [(target, source) for source, target in forward]
        low = lax.ppermute(
            lax.slice_in_dim(block, block.shape[dim] - width, None, axis=dim), axis, forward
        )
        high = lax.ppermute(lax.slice_in_dim(block, 0, width, axis=dim), axis, backward)
        block = jnp.concatenate([low, block, high], axis=dim)
    return block


def harmonic(first, second):
    total = first + second
    positive = total > 0.0
    return jnp.where(positive, 2.0 * first * second / jnp.where(positive, total, 1.0), 0.0)


def coefficients(conductivity, padded):
    return (
        4.0 * harmonic(conductivity, padded[2:, 1:-1, 1:-1]),
        4.0 * harmonic(conductivity, padded[:-2, 1:-1, 1:-1]),
        harmonic(conductivity, padded[1:-1, 2:, 1:-1]),
        harmonic(conductivity, padded[1:-1, :-2, 1:-1]),
        harmonic(conductivity, padded[1:-1, 1:-1, 2:]),
        harmonic(conductivity, padded[1:-1, 1:-1, :-2]),
    )


def apply_operator(field, faces, diag):
    padded = padded_2(field, (("east", 1), ("north", 2), ("layer", 0)), 1)
    beside = faces[0] * padded[2:, 1:-1, 1:-1] + faces[1] * padded[:-2, 1:-1, 1:-1]
    beside = beside + faces[2] * padded[1:-1, 2:, 1:-1] + faces[3] * padded[1:-1, :-2, 1:-1]
    beside = beside + faces[4] * padded[1:-1, 1:-1, 2:] + faces[5] * padded[1:-1, 1:-1, :-2]
    return diag * field - beside


def local_dot(first, second):
    return jnp.sum(first * second)


def precond_sum(residual, precond):
    return lax.psum(local_dot(residual, precond), ("east", "north", "layer"))


def per_device(recharge, conductivity, storage):
    cond_padded = padded_2(conductivity, (("east", 1), ("north", 2), ("layer", 0)), 1)
    faces = coefficients(conductivity, cond_padded)
    diag = storage + faces[0] + faces[1] + faces[2] + faces[3] + faces[4] + faces[5]
    diag = jnp.where(diag > 0.0, diag, 1.0)
    pressure = jnp.zeros_like(recharge)
    residual = recharge
    precond = residual / diag
    direction = precond
    rz_now = precond_sum(residual, precond)
    for step in range(ITERS):
        image = apply_operator(direction, faces, diag)
        alpha = rz_now / lax.psum(local_dot(direction, image), ("east", "north", "layer"))
        pressure = pressure + alpha * direction
        residual = residual - alpha * image
        if step + 1 < ITERS:
            precond = residual / diag
            rz_next = precond_sum(residual, precond)
            direction = precond + rz_next / rz_now * direction
            rz_now = rz_next
    return (pressure, residual)


def solution(mesh):
    placed = (P("layer", "east", "north"), P("layer", "east", "north"), P("layer", "east", "north"))
    return jax.shard_map(
        per_device,
        mesh=mesh,
        in_specs=placed,
        out_specs=(P("layer", "east", "north"), P("layer", "east", "north")),
        check_vma=False,
    )
```

profile of v0, /device:TPU:1, one launch (start us, length us, event | category | flops | bytes accessed | tf_op | source)
XLA Modules:
  0.0 417.5 jit_solution(16535821176860037328)
XLA Ops:
  1.4 4.0 collective-permute-start
  5.4 1.3 collective-permute-start.1
  6.8 3.0 collective-permute-done.1
  10.8 1.3 collective-permute-start.3
  12.1 4.1 collective-permute-start.2
  16.3 1.5 collective-permute-done.2
  17.9 1.3 collective-permute-start.5
  19.2 12.0 %collective-permute-start.4 = (f32[1,34,258]{2,1,0:T(8,128)S(1)}, f32[1,34,258]{2,1,0:T(8,128)S(1)}, u32[]{:S(2)}, u32[]{:S(2)}) collective-permute-start(f32[1,34,258]{2,1,0:T(8,128)S(1)} %get-tuple-element.21), channel_id=1, source_target_pairs={{1,0},{3,2},{5,4},{7,6},{9,8},{11,10},{13,12},{15,14},{17,16},{19,... | collective-permute-start | bytes 105272 | tf_op jit(solution)/shard_map/ppermute | solution.py:17
  32.4 1.4 collective-permute-start.6
  33.8 1.3 collective-permute-start.7
  35.1 3.0 collective-permute-done.7
  39.6 4.6 %collective-permute-start.8 = (f32[4,34,1]{2,1,0:T(8,128)S(1)}, f32[4,34,1]{2,1,0:T(8,128)S(1)}, u32[]{:S(2)}, u32[]{:S(2)}) collective-permute-start(f32[4,34,1]{2,1,0:T(8,128)S(1)} %get-tuple-element.25), channel_id=1, source_target_pairs={{0,2},{2,4},{4,6},{1,3},{3,5},{5,7},{8,10},{10,12},{12,14},{9,11},... | collective-permute-start | bytes 1640 | tf_op jit(solution)/shard_map/ppermute | solution.py:14
  44.2 1.5 collective-permute-done.8
  45.8 4.5 %collective-permute-start.10 = (f32[1,34,258]{2,1,0:T(8,128)S(1)}, f32[1,34,258]{2,1,0:T(8,128)S(1)}, u32[]{:S(2)}, u32[]{:S(2)}) collective-permute-start(f32[1,34,258]{2,1,0:T(8,128)S(1)} %get-tuple-element.18), channel_id=1, source_target_pairs={{1,0},{3,2},{5,4},{7,6},{9,8},{11,10},{13,12},{15,14},{17,16},{19,... | collective-permute-start | bytes 105272 | tf_op jit(solution)/shard_map/ppermute | solution.py:17
  50.3 1.3 collective-permute-start.11
  51.7 1.8 collective-permute-done.11
  54.5 118.7 %all-reduce = (f32[]{:T(128)}, f32[]{:T(128)}) all-reduce(f32[]{:T(128)} %get-tuple-element.3, f32[]{:T(128)} %get-tuple-element.2), channel_id=1, replica_groups=mesh['east'=96,'north'=4,'layer'=2] {'east','north','layer'}, use_global_device_ids=true, to_apply=%region_1.2 | all-reduce | flops 2 | bytes 16 | tf_op jit(solution)/shard_map/psum | solution.py:52
  175.2 103.7 %psum.30 = f32[]{:T(128)} all-reduce(f32[]{:T(128)} %get-tuple-element.8), channel_id=1, replica_groups=mesh['east'=96,'north'=4,'layer'=2] {'east','north','layer'}, use_global_device_ids=true, to_apply=%region_5.6 | all-reduce | flops 1 | bytes 8 | tf_op jit(solution)/shard_map/psum | solution.py:52
  282.8 3.0 collective-permute-done.13
  287.3 4.3 %collective-permute-start.14 = (f32[4,34,1]{2,1,0:T(8,128)S(1)}, f32[4,34,1]{2,1,0:T(8,128)S(1)}, u32[]{:S(2)}, u32[]{:S(2)}) collective-permute-start(f32[4,34,1]{2,1,0:T(8,128)S(1)} %get-tuple-element.23), channel_id=1, source_target_pairs={{0,2},{2,4},{4,6},{1,3},{3,5},{5,7},{8,10},{10,12},{12,14},{9,11},... | collective-permute-start | bytes 1640 | tf_op jit(solution)/shard_map/ppermute | solution.py:14
  291.6 1.5 collective-permute-done.14
  293.1 4.6 %collective-permute-start.16 = (f32[1,34,258]{2,1,0:T(8,128)S(1)}, f32[1,34,258]{2,1,0:T(8,128)S(1)}, u32[]{:S(2)}, u32[]{:S(2)}) collective-permute-start(f32[1,34,258]{2,1,0:T(8,128)S(1)} %get-tuple-element.16), channel_id=1, source_target_pairs={{1,0},{3,2},{5,4},{7,6},{9,8},{11,10},{13,12},{15,14},{17,16},{19,... | collective-permute-start | bytes 105272 | tf_op jit(solution)/shard_map/ppermute | solution.py:17
  299.1 1.8 collective-permute-done.17
  301.9 113.5 %psum.31 = f32[]{:T(128)} all-reduce(f32[]{:T(128)} %get-tuple-element.6), channel_id=1, replica_groups=mesh['east'=96,'north'=4,'layer'=2] {'east','north','layer'}, use_global_device_ids=true, to_apply=%region_7.8 | all-reduce | flops 1 | bytes 8 | tf_op jit(solution)/shard_map/psum | solution.py:67
  (39 shorter events, 13.5 us)
Async XLA Ops:
  1.4 5.3 %collective-permute-start = (f32[4,1,256]{2,1,0:T(1,128)S(1)}, f32[4,1,256]{2,1,0:T(1,128)S(1)}, u32[]{:S(2)}, u32[]{:S(2)}) collective-permute-start(f32[4,1,256]{2,1,0:T(1,128)S(1)} %get-tuple-element.32), channel_id=1, source_target_pairs={{0,8},{8,16},{16,24},{24,32},{32,40},{40,48},{48,56},{56,64},{64,7... | collective-permute-start | bytes 12296 | tf_op jit(solution)/shard_map/ppermute | solution.py:14
  5.4 4.4 %collective-permute-start.1 = (f32[4,1,256]{2,1,0:T(1,128)S(1)}, f32[4,1,256]{2,1,0:T(1,128)S(1)}, u32[]{:S(2)}, u32[]{:S(2)}) collective-permute-start(f32[4,1,256]{2,1,0:T(1,128)S(1)} %get-tuple-element.33), channel_id=1, source_target_pairs={{8,0},{16,8},{24,16},{32,24},{40,32},{48,40},{56,48},{64,56},{72,6... | collective-permute-start | bytes 12296 | tf_op jit(solution)/shard_map/ppermute | solution.py:17
  10.7 7.0 %copy-start = (f32[4,32,256]{2,1,0:T(8,128)S(1)}, f32[4,32,256]{2,1,0:T(8,128)}, u32[]{:S(2)}) copy-start(f32[4,32,256]{2,1,0:T(8,128)} %param.4) | copy-start | bytes 393220
  10.8 5.5 %collective-permute-start.3 = (f32[4,34,1]{2,1,0:T(8,128)S(1)}, f32[4,34,1]{2,1,0:T(8,128)S(1)}, u32[]{:S(2)}, u32[]{:S(2)}) collective-permute-start(f32[4,34,1]{2,1,0:T(8,128)S(1)} %get-tuple-element.26), channel_id=1, source_target_pairs={{2,0},{4,2},{6,4},{3,1},{5,3},{7,5},{10,8},{12,10},{14,12},{11,9},... | collective-permute-start | bytes 1640 | tf_op jit(solution)/shard_map/ppermute | solution.py:17
  12.1 19.9 %copy-start.1 = (f32[4,32,256]{2,1,0:T(8,128)S(1)}, f32[4,32,256]{2,1,0:T(8,128)}, u32[]{:S(2)}) copy-start(f32[4,32,256]{2,1,0:T(8,128)} %param.3) | copy-start | bytes 393220
  12.1 19.9 %copy-start.2 = (f32[4,32,256]{2,1,0:T(8,128)S(1)}, f32[4,32,256]{2,1,0:T(8,128)}, u32[]{:S(2)}) copy-start(f32[4,32,256]{2,1,0:T(8,128)} %param.5) | copy-start | bytes 393220
  12.1 5.6 %collective-permute-start.2 = (f32[4,34,1]{2,1,0:T(8,128)S(1)}, f32[4,34,1]{2,1,0:T(8,128)S(1)}, u32[]{:S(2)}, u32[]{:S(2)}) collective-permute-start(f32[4,34,1]{2,1,0:T(8,128)S(1)} %get-tuple-element.27), channel_id=1, source_target_pairs={{0,2},{2,4},{4,6},{1,3},{3,5},{5,7},{8,10},{10,12},{12,14},{9,11},... | collective-permute-start | bytes 1640 | tf_op jit(solution)/shard_map/ppermute | solution.py:14
  17.9 13.3 %collective-permute-start.5 = (f32[1,34,258]{2,1,0:T(8,128)S(1)}, f32[1,34,258]{2,1,0:T(8,128)S(1)}, u32[]{:S(2)}, u32[]{:S(2)}) collective-permute-start(f32[1,34,258]{2,1,0:T(8,128)S(1)} %get-tuple-element.20), channel_id=1, source_target_pairs={{0,1},{2,3},{4,5},{6,7},{8,9},{10,11},{12,13},{14,15},{16,17},{18,... | collective-permute-start | bytes 105272 | tf_op jit(solution)/shard_map/ppermute | solution.py:14
  19.2 12.9 %collective-permute-start.4 = (f32[1,34,258]{2,1,0:T(8,128)S(1)}, f32[1,34,258]{2,1,0:T(8,128)S(1)}, u32[]{:S(2)}, u32[]{:S(2)}) collective-permute-start(f32[1,34,258]{2,1,0:T(8,128)S(1)} %get-tuple-element.21), channel_id=1, source_target_pairs={{1,0},{3,2},{5,4},{7,6},{9,8},{11,10},{13,12},{15,14},{17,16},{19,... | collective-permute-start | bytes 105272 | tf_op jit(solution)/shard_map/ppermute | solution.py:17
  32.4 2.7 collective-permute-start.6
  33.8 4.4 %collective-permute-start.7 = (f32[4,1,256]{2,1,0:T(1,128)S(1)}, f32[4,1,256]{2,1,0:T(1,128)S(1)}, u32[]{:S(2)}, u32[]{:S(2)}) collective-permute-start(f32[4,1,256]{2,1,0:T(1,128)S(1)} %get-tuple-element.31), channel_id=1, source_target_pairs={{8,0},{16,8},{24,16},{32,24},{40,32},{48,40},{56,48},{64,56},{72,6... | collective-permute-start | bytes 12296 | tf_op jit(solution)/shard_map/ppermute | solution.py:17
  38.3 5.9 %collective-permute-start.9 = (f32[4,34,1]{2,1,0:T(8,128)S(1)}, f32[4,34,1]{2,1,0:T(8,128)S(1)}, u32[]{:S(2)}, u32[]{:S(2)}) collective-permute-start(f32[4,34,1]{2,1,0:T(8,128)S(1)} %get-tuple-element.24), channel_id=1, source_target_pairs={{2,0},{4,2},{6,4},{3,1},{5,3},{7,5},{10,8},{12,10},{14,12},{11,9},... | collective-permute-start | bytes 1640 | tf_op jit(solution)/shard_map/ppermute | solution.py:17
  39.6 6.1 %collective-permute-start.8 = (f32[4,34,1]{2,1,0:T(8,128)S(1)}, f32[4,34,1]{2,1,0:T(8,128)S(1)}, u32[]{:S(2)}, u32[]{:S(2)}) collective-permute-start(f32[4,34,1]{2,1,0:T(8,128)S(1)} %get-tuple-element.25), channel_id=1, source_target_pairs={{0,2},{2,4},{4,6},{1,3},{3,5},{5,7},{8,10},{10,12},{12,14},{9,11},... | collective-permute-start | bytes 1640 | tf_op jit(solution)/shard_map/ppermute | solution.py:14
  45.8 5.9 %collective-permute-start.10 = (f32[1,34,258]{2,1,0:T(8,128)S(1)}, f32[1,34,258]{2,1,0:T(8,128)S(1)}, u32[]{:S(2)}, u32[]{:S(2)}) collective-permute-start(f32[1,34,258]{2,1,0:T(8,128)S(1)} %get-tuple-element.18), channel_id=1, source_target_pairs={{1,0},{3,2},{5,4},{7,6},{9,8},{11,10},{13,12},{15,14},{17,16},{19,... | collective-permute-start | bytes 105272 | tf_op jit(solution)/shard_map/ppermute | solution.py:17
  50.3 3.1 collective-permute-start.11
  280.2 2.6 collective-permute-start.12
  281.5 4.4 %collective-permute-start.13 = (f32[4,1,256]{2,1,0:T(1,128)S(1)}, f32[4,1,256]{2,1,0:T(1,128)S(1)}, u32[]{:S(2)}, u32[]{:S(2)}) collective-permute-start(f32[4,1,256]{2,1,0:T(1,128)S(1)} %get-tuple-element.29), channel_id=1, source_target_pairs={{8,0},{16,8},{24,16},{32,24},{40,32},{48,40},{56,48},{64,56},{72,6... | collective-permute-start | bytes 12296 | tf_op jit(solution)/shard_map/ppermute | solution.py:17
  286.0 5.6 %collective-permute-start.15 = (f32[4,34,1]{2,1,0:T(8,128)S(1)}, f32[4,34,1]{2,1,0:T(8,128)S(1)}, u32[]{:S(2)}, u32[]{:S(2)}) collective-permute-start(f32[4,34,1]{2,1,0:T(8,128)S(1)} %get-tuple-element.22), channel_id=1, source_target_pairs={{2,0},{4,2},{6,4},{3,1},{5,3},{7,5},{10,8},{12,10},{14,12},{11,9},... | collective-permute-start | bytes 1640 | tf_op jit(solution)/shard_map/ppermute | solution.py:17
  287.3 5.8 %collective-permute-start.14 = (f32[4,34,1]{2,1,0:T(8,128)S(1)}, f32[4,34,1]{2,1,0:T(8,128)S(1)}, u32[]{:S(2)}, u32[]{:S(2)}) collective-permute-start(f32[4,34,1]{2,1,0:T(8,128)S(1)} %get-tuple-element.23), channel_id=1, source_target_pairs={{0,2},{2,4},{4,6},{1,3},{3,5},{5,7},{8,10},{10,12},{12,14},{9,11},... | collective-permute-start | bytes 1640 | tf_op jit(solution)/shard_map/ppermute | solution.py:14
  293.1 5.9 %collective-permute-start.16 = (f32[1,34,258]{2,1,0:T(8,128)S(1)}, f32[1,34,258]{2,1,0:T(8,128)S(1)}, u32[]{:S(2)}, u32[]{:S(2)}) collective-permute-start(f32[1,34,258]{2,1,0:T(8,128)S(1)} %get-tuple-element.16), channel_id=1, source_target_pairs={{1,0},{3,2},{5,4},{7,6},{9,8},{11,10},{13,12},{15,14},{17,16},{19,... | collective-permute-start | bytes 105272 | tf_op jit(solution)/shard_map/ppermute | solution.py:17
  297.7 3.1 collective-permute-start.17
where the time goes:
time: 418 us; the launch traced here: 417 us
  blocking collectives  336 us (80%)
  starting transfers between devices  52.4 us (13%)
  waiting for transfers between devices  18 us (4%)
  other arithmetic  5.08 us (1%)
  between operations  4.96 us (1%)
    psum x2, blocking collectives, precond_sum(): return lax.psum(local_dot(residual, precond), ('east', 'north', 'layer'))  222 us
    psum x1, blocking collectives, per_device(): lax.psum(local_dot(direction, image), ('east', 'north', 'layer'))  114 us
    ppermute x9, starting transfers between devices, padded_2(): lax.ppermute(lax.slice_in_dim(block, 0, width, axis=dim), axis, backward)  28.8 us
    ppermute x9, starting transfers between devices, padded_2(): lax.ppermute(lax.slice_in_dim(block, block.shape[dim] - width, None, axis...  23.6 us
    ppermute x9, waiting for transfers between devices, padded_2(): lax.ppermute(lax.slice_in_dim(block, 0, width, axis=dim), axis, backward)  10 us
  transfers between devices with their start and end apart: 18, of which 9 were waited for; matrix products, arithmetic and copies ran while one was open for 0% of the time, Pallas kernels for 0%

commit v1 on v0

v1 whole, which is shorter than its diff:
```python
import jax
import jax.numpy as jnp
from jax import lax
from jax.experimental import pallas as pl
from jax.experimental.pallas import tpu as pltpu
from jax.sharding import Mesh, PartitionSpec as P

EAST = ("z", "y")
ALL = ("z", "y", "x", "c")
F32 = jnp.float32

NK, NR = 7, 6
SLABS = NK + 2 * NR
SIDE = [("k", j) for j in range(6)] + [("r", j) for j in range(5)] + [("s", j) for j in range(5)]
SIDE_AT = {name: i for i, name in enumerate(SIDE)}


def slab_index(name, j):
    return {"k": 0, "r": NK, "s": NK + NR}[name] + j


def pack_layer(r_ref, k_ref, s_ref, own_ref, out_ref):
    core = lax.axis_index("c")
    at = 0
    for base, ref, count in ((0, k_ref, 3), (4, r_ref, 2), (8, s_ref, 2)):
        for j in range(4):
            own_ref[base + j] = ref[jnp.where(core == 0, j, 3 - j)]
        for j in range(count):
            out_ref[at] = ref[jnp.where(core == 0, 3 - j, j)]
            at += 1


def main_slab(own_ref, in_ref, name, j):
    base, beside = {"k": (0, 0), "r": (4, 3), "s": (8, 5)}[name]
    return own_ref[base + j] if j < 4 else in_ref[beside + j - 4]


def pack_north(own_ref, in_ref, low_ref, high_ref):
    lane = lax.broadcasted_iota(jnp.int32, (32, 128), 1)
    low = jnp.zeros((32, 128), F32)
    high = jnp.zeros((32, 128), F32)
    for i, (name, j) in enumerate(SIDE):
        slab = main_slab(own_ref, in_ref, name, j)
        mine = (lane >= 3 * i) & (lane < 3 * i + 3)
        low = jnp.where(mine, pltpu.roll(slab[:, :128], 3 * i, 1) if i else slab[:, :128], low)
        high = jnp.where(mine, pltpu.roll(slab[:, 128:], 3 * i + 3, 1), high)
    low_ref[...] = low
    high_ref[...] = high


def pack_east(own_ref, in_ref, from_low_ref, from_high_ref, wide_ref, low_ref, high_ref):
    lane = lax.broadcasted_iota(jnp.int32, (32, 128), 1)
    from_low, from_high = from_low_ref[...], from_high_ref[...]
    for name, count in (("k", NK), ("r", NR), ("s", NR)):
        for j in range(count):
            at = slab_index(name, j)
            wide_ref[at, :, :256] = main_slab(own_ref, in_ref, name, j)
            beyond = jnp.zeros((32, 128), F32)
            if (name, j) in SIDE_AT:
                i = SIDE_AT[name, j]
                above = pltpu.roll(from_high, 128 - 3 * i, 1) if i else from_high
                below = pltpu.roll(from_low, 125 - 3 * i, 1)
                beyond = jnp.where(lane < 3, above, jnp.where(lane >= 125, below, 0.0))
            wide_ref[at, :, 256:] = beyond
    row = lax.broadcasted_iota(jnp.int32, (8, 384), 0)
    for j in range(6):
        low, high = wide_ref[j, 0:8, :], wide_ref[j, 24:32, :]
        if j < 5:
            r, s = slab_index("r", j), slab_index("s", j)
            low = jnp.where(row < 3, low, jnp.where(row < 5, pltpu.roll(wide_ref[r, 0:8, :], 3, 0), pltpu.roll(wide_ref[s, 0:8, :], 5, 0)))
            high = jnp.where(row >= 5, high, jnp.where(row >= 3, pltpu.roll(wide_ref[r, 24:32, :], 5, 0), pltpu.roll(wide_ref[s, 24:32, :], 3, 0)))
        low_ref[j] = low
        high_ref[j] = high


def harmonic(first, second):
    return 2.0 * first * second / jnp.maximum(first + second, 1e-30)


def operate(wide_ref, from_low_ref, from_high_ref, z_ref, q_ref, w_ref, u_ref, sums_ref):
    row = lax.broadcasted_iota(jnp.int32, (8, 384), 0)

    def whole(name, j):
        main = wide_ref[slab_index(name, j)]
        if (name, j) not in SIDE_AT:
            beyond = jnp.zeros((8, 384), F32)
        else:
            above, below = from_high_ref[j], from_low_ref[j]
            if name == "k":
                beyond = jnp.where(row < 3, above, jnp.where(row >= 5, below, 0.0))
            else:
                up, down = (5, 3) if name == "r" else (3, 5)
                beyond = jnp.where(row < 2, pltpu.roll(above, up, 0), jnp.where(row >= 6, pltpu.roll(below, down, 0), 0.0))
        return jnp.concatenate([main, beyond], axis=0)

    def north(v):
        return pltpu.roll(v, 383, 1)

    def south(v):
        return pltpu.roll(v, 1, 1)

    def east(v):
        return pltpu.roll(v, 39, 0)

    def west(v):
        return pltpu.roll(v, 1, 0)

    k = [whole("k", j) for j in range(NK)]
    face_l = [4.0 * harmonic(k[j], k[j + 1]) for j in range(NR)]
    face_e = [harmonic(k[j], east(k[j])) for j in range(NR)]
    face_n = [harmonic(k[j], north(k[j])) for j in range(NR)]
    diag, z = [], []
    for j in range(NR):
        d = whole("s", j) + face_l[j] + face_e[j] + west(face_e[j]) + face_n[j] + south(face_n[j])
        if j:
            d = d + face_l[j - 1]
        d = jnp.where(d > 0.0, d, 1.0)
        diag.append(d)
        z.append(whole("r", j) / d)

    def apply(v, count):
        out = []
        for j in range(count):
            beside = face_l[j] * v[j + 1] + face_e[j] * east(v[j]) + west(face_e[j] * v[j])
            beside = beside + face_n[j] * north(v[j]) + south(face_n[j] * v[j])
            if j:
                beside = beside + face_l[j - 1] * v[j - 1]
            out.append(diag[j] * v[j] - beside)
        return out

    q = apply(z, 5)
    w = [q[j] / diag[j] for j in range(5)]
    u = apply(w, 4)
    totals = [jnp.zeros((8, 128), F32)] * 4
    for j in range(4):
        own = [v[j][:32, :256] for v in (z, q, w, u)]
        for ref, v in zip((z_ref, q_ref, w_ref, u_ref), own):
            ref[j] = v
        zo, qo, wo, uo = own
        rz = wide_ref[slab_index("r", j), :, :256] * zo
        for i, product in enumerate((rz, zo * qo, qo * wo, wo * uo)):
            for a in range(4):
                for b in range(2):
                    totals[i] = totals[i] + product[8 * a : 8 * a + 8, 128 * b : 128 * b + 128]
    lane = lax.broadcasted_iota(jnp.int32, (1, 128), 1)
    line = jnp.zeros((1, 128), F32)
    for i in range(4):
        line = jnp.where(lane == i, jnp.sum(totals[i]), line)
    for i in range(sums_ref.shape[0]):
        sums_ref[i] = line


def finish(sums_ref, r_ref, z_ref, q_ref, w_ref, u_ref, pressure_ref, residual_ref):
    core = lax.axis_index("c")
    line = sums_ref[0]
    for i in range(1, sums_ref.shape[0]):
        line = line + sums_ref[i]
    lane = lax.broadcasted_iota(jnp.int32, (1, 128), 1)
    rz, zq, qw, wu = (jnp.sum(jnp.where(lane == i, line, 0.0), axis=1, keepdims=True) for i in range(4))
    alpha = rz / zq
    rz_next = alpha * alpha * qw - rz
    grown = 1.0 + rz_next / rz
    curve = grown * grown * zq - 2.0 * grown * alpha * qw + alpha * alpha * wu
    alpha_next = rz_next / curve
    along = alpha + alpha_next * grown
    across = alpha * alpha_next
    for j in range(4):
        to = jnp.where(core == 0, j, 3 - j)
        pressure_ref[to] = along * z_ref[j] - across * w_ref[j]
        residual_ref[to] = r_ref[4 + j] - along * q_ref[j] + across * u_ref[j]


def call(kernel, *shapes):
    in_vmem = pl.BlockSpec(memory_space=pltpu.VMEM)

    def run(*args):
        return pl.pallas_call(
            kernel,
            out_shape=[jax.ShapeDtypeStruct(shape, F32) for shape in shapes],
            in_specs=[in_vmem] * len(args),
            out_specs=[in_vmem] * len(shapes),
            compiler_params=pltpu.CompilerParams(vmem_limit_bytes=32 * 1024 * 1024),
        )(*args)

    return run


def chain(count):
    up = [(i, i + 1) for i in range(count - 1)]
    return up, [(target, source) for source, target in up]


def spread_sum(line, axes, count):
    return lax.all_to_all(jnp.broadcast_to(line[None], (count, 1, 128)), axes, 0, 0)


def per_device(recharge, conductivity, storage):
    size = {axis: lax.axis_size(axis) for axis in ALL}
    own, out = call(pack_layer, (12, 32, 256), (7, 32, 256))(recharge, conductivity, storage)
    beside = lax.ppermute(out, "c", [(0, 1), (1, 0)])
    low, high = call(pack_north, (32, 128), (32, 128))(own, beside)
    up, down = chain(size["x"])
    from_low, from_high = lax.ppermute(high, "x", up), lax.ppermute(low, "x", down)
    wide, low, high = call(pack_east, (SLABS, 32, 384), (6, 8, 384), (6, 8, 384))(own, beside, from_low, from_high)
    up, down = chain(size["z"] * size["y"])
    from_low, from_high = lax.ppermute(high, EAST, up), lax.ppermute(low, EAST, down)
    first = size["y"] * size["x"]
    block = (4, 32, 256)
    z, q, w, u, sums = call(operate, block, block, block, block, (first, 1, 128))(wide, from_low, from_high)
    sums = lax.all_to_all(sums, ("y", "x"), 0, 0)
    sums = spread_sum(jnp.sum(sums, axis=0), ("z", "c"), size["z"] * size["c"])
    return tuple(call(finish, block, block)(sums, own, z, q, w, u))


def solution(mesh):
    east, north, layer = (mesh.shape[axis] for axis in ("east", "north", "layer"))
    row = 8 if east % 8 == 0 else 1
    fine = Mesh(mesh.devices.reshape(east // row, row, north, layer), ALL)
    placed = P("c", EAST, "x")
    return jax.shard_map(
        per_device, mesh=fine, in_specs=(placed,) * 3, out_specs=(placed,) * 2, check_vma=False
    )
```

time: 418 us -> 73.4 us (0.18)
  blocking collectives: 336 us -> 41.7 us
  starting transfers between devices: 52.4 us -> 17.6 us
  waiting for transfers between devices: 18 us -> 8.07 us
  other arithmetic: 5.08 us -> 0.05 us
  between operations: 4.96 us -> 0.71 us
    psum x3 -> x0, blocking collectives: 336 us -> none  [the longest x2 222 us: precond_sum(): return lax.psum(local_dot(residual, precond), ('east', 'north', 'layer'))]
    all_to_all x0 -> x2, blocking collectives: none -> 41.7 us  [the longest x1 29.1 us: spread_sum(): lax.all_to_all(jnp.broadcast_to(line[None], (count, 1, 128)), axes, 0, 0)]
    ppermute x18 -> x5, starting transfers between devices: 52.4 us -> 17.6 us  [the longest x1 12.4 us: per_device(): beside = lax.ppermute(out, 'c', [(0, 1), (1, 0)])]
    ppermute x18 -> x5, waiting for transfers between devices: 18 us -> 8.07 us  [the longest x1 3.71 us: per_device(): lax.ppermute(low, EAST, down)]
  transfers between devices with their start and end apart: 18 -> 5, of which waited for: 9 -> 4; matrix products, arithmetic and copies ran while one was open for 0% -> 0% of each run, Pallas kernels for 0% -> 0%
where the time goes in v1:
time: 73.4 us; the launch traced here: 73 us
  blocking collectives  41.7 us (57%)
  starting transfers between devices  17.6 us (24%)
  waiting for transfers between devices  8.07 us (11%)
  local copies, waits for them, and re-layouts  2.72 us (4%)
  Pallas kernels  2.16 us (3%)
    all_to_all x1, blocking collectives, spread_sum(): lax.all_to_all(jnp.broadcast_to(line[None], (count, 1, 128)), axes, 0, 0)  29.1 us
    all_to_all x1, blocking collectives, per_device(): sums = lax.all_to_all(sums, ('y', 'x'), 0, 0)  12.7 us
    ppermute x1, starting transfers between devices, per_device(): beside = lax.ppermute(out, 'c', [(0, 1), (1, 0)])  12.4 us
    ppermute x1, waiting for transfers between devices, per_device(): lax.ppermute(low, EAST, down)  3.71 us
    ppermute x1, waiting for transfers between devices, per_device(): lax.ppermute(low, 'x', down)  3.17 us
    unnamed x6, local copies, waits for them, and re-layouts  2.7 us
    pallas_call x5, Pallas kernels, run(): pl.pallas_call(kernel, out_shape=[jax.ShapeDtypeStruct(shape, F32) for sh...  2.16 us
  transfers between devices with their start and end apart: 5, of which 4 were waited for; matrix products, arithmetic and copies ran while one was open for 0% of the time, Pallas kernels for 0%

profile of v1, /device:TPU:1, one launch (start us, length us, event | category | flops | bytes accessed | tf_op | source)
XLA Modules:
  0.0 73.0 jit_solution(15853498329372910922)
XLA Ops:
  0.6 0.0 copy-start
  0.6 0.9 %copy-done = f32[4,32,256]{2,1,0:T(8,128)S(1)} copy-done((f32[4,32,256]{2,1,0:T(8,128)S(1)}, f32[4,32,256]{2,1,0:T(8,128)}, u32[]{:S(2)}) %copy-start) | copy-done | bytes 131096
  1.5 0.0 copy-start.1
  1.5 0.9 %copy-done.1 = f32[4,32,256]{2,1,0:T(8,128)S(1)} copy-done((f32[4,32,256]{2,1,0:T(8,128)S(1)}, f32[4,32,256]{2,1,0:T(8,128)}, u32[]{:S(2)}) %copy-start.1) | copy-done | bytes 131096
  2.4 0.0 copy-start.2
  2.4 0.9 %copy-done.2 = f32[4,32,256]{2,1,0:T(8,128)S(1)} copy-done((f32[4,32,256]{2,1,0:T(8,128)S(1)}, f32[4,32,256]{2,1,0:T(8,128)}, u32[]{:S(2)}) %copy-start.2) | copy-done | bytes 131096
  3.4 12.4 %collective-permute-start = (f32[7,32,256]{2,1,0:T(8,128)S(1)}, f32[7,32,256]{2,1,0:T(8,128)S(1)}, u32[]{:S(2)}, u32[]{:S(2)}) collective-permute-start(f32[7,32,256]{2,1,0:T(8,128)S(1)} %get-tuple-element.15), channel_id=1, source_target_pairs={{0,1},{1,0},{2,3},{3,2},{4,5},{5,4},{6,7},{7,6},{8,9},{9,8},{10,11... | collective-permute-start | bytes 688136 | tf_op jit(solution)/shard_map/ppermute | solution.py:200
  15.8 1.1 %collective-permute-done.in_ref = f32[7,32,256]{2,1,0:T(8,128)S(1)} collective-permute-done((f32[7,32,256]{2,1,0:T(8,128)S(1)}, f32[7,32,256]{2,1,0:T(8,128)S(1)}, u32[]{:S(2)}, u32[]{:S(2)}) %collective-permute-start) | collective-permute-done | bytes 229408 | tf_op jit(solution)/shard_map/ppermute | solution.py:200
  16.9 0.2 shard_map.51
  17.1 1.3 %collective-permute-start.1 = (f32[32,128]{1,0:T(8,128)S(1)}, f32[32,128]{1,0:T(8,128)S(1)}, u32[]{:S(2)}, u32[]{:S(2)}) collective-permute-start(f32[32,128]{1,0:T(8,128)S(1)} %get-tuple-element.16), channel_id=1, source_target_pairs={{0,2},{2,4},{4,6},{1,3},{3,5},{5,7},{8,10},{10,12},{12,14},{9,11},... | collective-permute-start | bytes 49160 | tf_op jit(solution)/shard_map/ppermute | solution.py:203
  18.4 1.3 %collective-permute-start.2 = (f32[32,128]{1,0:T(8,128)S(1)}, f32[32,128]{1,0:T(8,128)S(1)}, u32[]{:S(2)}, u32[]{:S(2)}) collective-permute-start(f32[32,128]{1,0:T(8,128)S(1)} %get-tuple-element.17), channel_id=1, source_target_pairs={{2,0},{4,2},{6,4},{3,1},{5,3},{7,5},{10,8},{12,10},{14,12},{11,9},... | collective-permute-start | bytes 49160 | tf_op jit(solution)/shard_map/ppermute | solution.py:203
  19.7 0.0 collective-permute-done.1.from_low_ref
  19.7 3.2 %collective-permute-done.2.from_high_ref = f32[32,128]{1,0:T(8,128)S(1)} collective-permute-done((f32[32,128]{1,0:T(8,128)S(1)}, f32[32,128]{1,0:T(8,128)S(1)}, u32[]{:S(2)}, u32[]{:S(2)}) %collective-permute-start.2) | collective-permute-done | bytes 16416 | tf_op jit(solution)/shard_map/ppermute | solution.py:203
  22.9 0.2 shard_map.52
  23.1 1.3 %collective-permute-start.3 = (f32[6,8,384]{2,1,0:T(8,128)S(1)}, f32[6,8,384]{2,1,0:T(8,128)S(1)}, u32[]{:S(2)}, u32[]{:S(2)}) collective-permute-start(f32[6,8,384]{2,1,0:T(8,128)S(1)} %get-tuple-element.19), channel_id=1, source_target_pairs={{0,8},{8,16},{16,24},{24,32},{32,40},{40,48},{48,56},{56,64},{64,7... | collective-permute-start | bytes 221192 | tf_op jit(solution)/shard_map/ppermute | solution.py:206
  24.4 1.3 %collective-permute-start.4 = (f32[6,8,384]{2,1,0:T(8,128)S(1)}, f32[6,8,384]{2,1,0:T(8,128)S(1)}, u32[]{:S(2)}, u32[]{:S(2)}) collective-permute-start(f32[6,8,384]{2,1,0:T(8,128)S(1)} %get-tuple-element.20), channel_id=1, source_target_pairs={{8,0},{16,8},{24,16},{32,24},{40,32},{48,40},{56,48},{64,56},{72,6... | collective-permute-start | bytes 221192 | tf_op jit(solution)/shard_map/ppermute | solution.py:206
  25.7 0.1 collective-permute-done.3.from_low_ref
  25.8 3.7 %collective-permute-done.4.from_high_ref = f32[6,8,384]{2,1,0:T(8,128)S(1)} collective-permute-done((f32[6,8,384]{2,1,0:T(8,128)S(1)}, f32[6,8,384]{2,1,0:T(8,128)S(1)}, u32[]{:S(2)}, u32[]{:S(2)}) %collective-permute-start.4) | collective-permute-done | bytes 73760 | tf_op jit(solution)/shard_map/ppermute | solution.py:206
  29.5 0.9 %shard_map.53 = (f32[4,32,256]{2,1,0:T(8,128)S(1)}, f32[4,32,256]{2,1,0:T(8,128)S(1)}, f32[4,32,256]{2,1,0:T(8,128)S(1)}, f32[4,32,256]{2,1,0:T(8,128)S(1)}, f32[32,1,128]{2,1,0:T(1,128)S(1)}) custom-call(f32[19,32,384]{2,1,0:T(8,128)S(1)} %get-tuple-element.18.wide_ref, f32[6,8,384]{2,1,0:T(8,128)S(1)} %collective-permute-done.3.from_low_ref, ...), custom_call_target="tpu_custom_call" | custom-call | tf_op jit(solution)/shard_map/pallas_call | solution.py:177
  30.4 12.7 %all_to_all.10 = f32[32,1,128]{2,1,0:T(1,128)S(1)} all-to-all(f32[32,1,128]{2,1,0:T(1,128)S(1)} %get-tuple-element.21), channel_id=1, replica_groups=mesh['z'=12,'y'=8,'x'=4,'c'=2] {'y','x'}, dimensions={0} | all-to-all | bytes 32768 | tf_op jit(solution)/shard_map/all_to_all | solution.py:210
  43.1 0.1 reduce_sum.9
  43.1 29.1 %all_to_all.11.sums_ref = f32[24,1,128]{2,1,0:T(1,128)S(1)} all-to-all(f32[24,1,128]{2,1,0:T(1,128)S(1)} %broadcast_in_dim.2), channel_id=1, replica_groups=mesh['z'=12,'y'=8,'x'=4,'c'=2] {'z','c'}, dimensions={0} | all-to-all | bytes 24576 | tf_op jit(solution)/shard_map/all_to_all | solution.py:194
  72.2 0.8 %shard_map.54 = (f32[4,32,256]{2,1,0:T(8,128)}, f32[4,32,256]{2,1,0:T(8,128)}) custom-call(f32[24,1,128]{2,1,0:T(1,128)S(1)} %all_to_all.11.sums_ref, f32[12,32,256]{2,1,0:T(8,128)S(1)} %get-tuple-element.14.own_ref.r_ref, f32[4,32,256]{2,1,0:T(8,128)S(1)} %get-tuple-element.22.z_ref, f32[4,32,256]{2,1,0:T(8,128)S(1)} %get-tuple-element.23.q_ref, ...), custom_call_target="tpu_custom_call" | custom-call | tf_op jit(solution)/shard_map/pallas_call | solution.py:177
  (2 shorter events, 0.1 us)
Async XLA Ops:
  0.6 0.9 %copy-start = (f32[4,32,256]{2,1,0:T(8,128)S(1)}, f32[4,32,256]{2,1,0:T(8,128)}, u32[]{:S(2)}) copy-start(f32[4,32,256]{2,1,0:T(8,128)} %r_ref.1) | copy-start | bytes 393220
  1.5 0.9 %copy-start.1 = (f32[4,32,256]{2,1,0:T(8,128)S(1)}, f32[4,32,256]{2,1,0:T(8,128)}, u32[]{:S(2)}) copy-start(f32[4,32,256]{2,1,0:T(8,128)} %k_ref.1) | copy-start | bytes 393220
  2.4 0.9 %copy-start.2 = (f32[4,32,256]{2,1,0:T(8,128)S(1)}, f32[4,32,256]{2,1,0:T(8,128)}, u32[]{:S(2)}) copy-start(f32[4,32,256]{2,1,0:T(8,128)} %s_ref.1) | copy-start | bytes 393220
  3.4 13.5 %collective-permute-start = (f32[7,32,256]{2,1,0:T(8,128)S(1)}, f32[7,32,256]{2,1,0:T(8,128)S(1)}, u32[]{:S(2)}, u32[]{:S(2)}) collective-permute-start(f32[7,32,256]{2,1,0:T(8,128)S(1)} %get-tuple-element.15), channel_id=1, source_target_pairs={{0,1},{1,0},{2,3},{3,2},{4,5},{5,4},{6,7},{7,6},{8,9},{9,8},{10,11... | collective-permute-start | bytes 688136 | tf_op jit(solution)/shard_map/ppermute | solution.py:200
  17.1 2.6 %collective-permute-start.1 = (f32[32,128]{1,0:T(8,128)S(1)}, f32[32,128]{1,0:T(8,128)S(1)}, u32[]{:S(2)}, u32[]{:S(2)}) collective-permute-start(f32[32,128]{1,0:T(8,128)S(1)} %get-tuple-element.16), channel_id=1, source_target_pairs={{0,2},{2,4},{4,6},{1,3},{3,5},{5,7},{8,10},{10,12},{12,14},{9,11},... | collective-permute-start | bytes 49160 | tf_op jit(solution)/shard_map/ppermute | solution.py:203
  18.4 4.5 %collective-permute-start.2 = (f32[32,128]{1,0:T(8,128)S(1)}, f32[32,128]{1,0:T(8,128)S(1)}, u32[]{:S(2)}, u32[]{:S(2)}) collective-permute-start(f32[32,128]{1,0:T(8,128)S(1)} %get-tuple-element.17), channel_id=1, source_target_pairs={{2,0},{4,2},{6,4},{3,1},{5,3},{7,5},{10,8},{12,10},{14,12},{11,9},... | collective-permute-start | bytes 49160 | tf_op jit(solution)/shard_map/ppermute | solution.py:203
  23.1 2.7 %collective-permute-start.3 = (f32[6,8,384]{2,1,0:T(8,128)S(1)}, f32[6,8,384]{2,1,0:T(8,128)S(1)}, u32[]{:S(2)}, u32[]{:S(2)}) collective-permute-start(f32[6,8,384]{2,1,0:T(8,128)S(1)} %get-tuple-element.19), channel_id=1, source_target_pairs={{0,8},{8,16},{16,24},{24,32},{32,40},{40,48},{48,56},{56,64},{64,7... | collective-permute-start | bytes 221192 | tf_op jit(solution)/shard_map/ppermute | solution.py:206
  24.4 5.1 %collective-permute-start.4 = (f32[6,8,384]{2,1,0:T(8,128)S(1)}, f32[6,8,384]{2,1,0:T(8,128)S(1)}, u32[]{:S(2)}, u32[]{:S(2)}) collective-permute-start(f32[6,8,384]{2,1,0:T(8,128)S(1)} %get-tuple-element.20), channel_id=1, source_target_pairs={{8,0},{16,8},{24,16},{32,24},{40,32},{48,40},{56,48},{64,56},{72,6... | collective-permute-start | bytes 221192 | tf_op jit(solution)/shard_map/ppermute | solution.py:206

commit v2 on v1

--- a/solution.py
+++ b/solution.py
@@ -1,3 +1,5 @@
+import functools
+
 import jax
 import jax.numpy as jnp
 from jax import lax
@@ -12,55 +14,66 @@
 NK, NR = 7, 6
 SLABS = NK + 2 * NR
 SIDE = [("k", j) for j in range(6)] + [("r", j) for j in range(5)] + [("s", j) for j in range(5)]
-SIDE_AT = {name: i for i, name in enumerate(SIDE)}
+OWN = {"k": 0, "r": 4, "s": 8}
+HALF = 64
 
 
 def slab_index(name, j):
     return {"k": 0, "r": NK, "s": NK + NR}[name] + j
 
 
-def pack_layer(r_ref, k_ref, s_ref, own_ref, out_ref):
+def pack_own(r_hbm, k_hbm, s_hbm, own_ref, out_ref, side_ref, r_ref, k_ref, s_ref, arrived):
+    copies = [
+        pltpu.make_async_copy(source, target, arrived.at[i])
+        for i, (source, target) in enumerate(((k_hbm, k_ref), (r_hbm, r_ref), (s_hbm, s_ref)))
+    ]
+    for copy in copies:
+        copy.start()
     core = lax.axis_index("c")
+    lane = lax.broadcasted_iota(jnp.int32, (32, 128), 1)
+    line = jnp.zeros((32, 128), F32)
     at = 0
-    for base, ref, count in ((0, k_ref, 3), (4, r_ref, 2), (8, s_ref, 2)):
+    for copy, ref, name, count in zip(copies, (k_ref, r_ref, s_ref), "krs", (3, 2, 2)):
+        copy.wait()
         for j in range(4):
-            own_ref[base + j] = ref[jnp.where(core == 0, j, 3 - j)]
+            slab = ref[jnp.where(core == 0, j, 3 - j)]
+            i = OWN[name] + j
+            own_ref[i] = slab
+            low, high = slab[:, :128], pltpu.roll(slab[:, 128:], 3 * i + HALF + 3, 1)
+            low = pltpu.roll(low, 3 * i, 1) if i else low
+            line = jnp.where((lane >= 3 * i) & (lane < 3 * i + 3), low, line)
+            line = jnp.where((lane >= HALF + 3 * i) & (lane < HALF + 3 * i + 3), high, line)
         for j in range(count):
             out_ref[at] = ref[jnp.where(core == 0, 3 - j, j)]
             at += 1
+    for i in range(side_ref.shape[0]):
+        side_ref[i] = line
 
 
 def main_slab(own_ref, in_ref, name, j):
-    base, beside = {"k": (0, 0), "r": (4, 3), "s": (8, 5)}[name]
-    return own_ref[base + j] if j < 4 else in_ref[beside + j - 4]
-
-
-def pack_north(own_ref, in_ref, low_ref, high_ref):
+    beside = {"k": 0, "r": 3, "s": 5}[name]
+    return own_ref[OWN[name] + j] if j < 4 else in_ref[beside + j - 4]
+
+
+def pack_east(north_count, own_ref, in_ref, side_ref, wide_ref, low_ref, high_ref):
     lane = lax.broadcasted_iota(jnp.int32, (32, 128), 1)
-    low = jnp.zeros((32, 128), F32)
-    high = jnp.zeros((32, 128), F32)
-    for i, (name, j) in enumerate(SIDE):
-        slab = main_slab(own_ref, in_ref, name, j)
-        mine = (lane >= 3 * i) & (lane < 3 * i + 3)
-        low = jnp.where(mine, pltpu.roll(slab[:, :128], 3 * i, 1) if i else slab[:, :128], low)
-        high = jnp.where(mine, pltpu.roll(slab[:, 128:], 3 * i + 3, 1), high)
-    low_ref[...] = low
-    high_ref[...] = high
-
-
-def pack_east(own_ref, in_ref, from_low_ref, from_high_ref, wide_ref, low_ref, high_ref):
-    lane = lax.broadcasted_iota(jnp.int32, (32, 128), 1)
-    from_low, from_high = from_low_ref[...], from_high_ref[...]
+    core, place = lax.axis_index("c"), lax.axis_index("x")
+    up, down = jnp.minimum(place + 1, north_count - 1), jnp.maximum(place - 1, 0)
+    has_up, has_down = place < north_count - 1, place > 0
+    same = (side_ref[2 * up + core], side_ref[2 * down + core])
+    other = (side_ref[2 * up + 1 - core], side_ref[2 * down + 1 - core])
+    take_up, take_down = (lane < 3) & has_up, (lane >= 125) & has_down
     for name, count in (("k", NK), ("r", NR), ("s", NR)):
         for j in range(count):
             at = slab_index(name, j)
             wide_ref[at, :, :256] = main_slab(own_ref, in_ref, name, j)
             beyond = jnp.zeros((32, 128), F32)
-            if (name, j) in SIDE_AT:
-                i = SIDE_AT[name, j]
-                above = pltpu.roll(from_high, 128 - 3 * i, 1) if i else from_high
-                below = pltpu.roll(from_low, 125 - 3 * i, 1)
-                beyond = jnp.where(lane < 3, above, jnp.where(lane >= 125, below, 0.0))
+            if (name, j) in SIDE:
+                above, below = same if j < 4 else other
+                i = OWN[name] + (j if j < 4 else 7 - j)
+                above = pltpu.roll(above, 128 - 3 * i, 1) if i else above
+                below = pltpu.roll(below, (125 - HALF - 3 * i) % 128, 1)
+                beyond = jnp.where(take_up, above, jnp.where(take_down, below, 0.0))
             wide_ref[at, :, 256:] = beyond
     row = lax.broadcasted_iota(jnp.int32, (8, 384), 0)
     for j in range(6):
@@ -82,7 +95,7 @@
 
     def whole(name, j):
         main = wide_ref[slab_index(name, j)]
-        if (name, j) not in SIDE_AT:
+        if (name, j) not in SIDE:
             beyond = jnp.zeros((8, 384), F32)
         else:
             above, below = from_high_ref[j], from_low_ref[j]
@@ -170,16 +183,15 @@
         residual_ref[to] = r_ref[4 + j] - along * q_ref[j] + across * u_ref[j]
 
 
-def call(kernel, *shapes):
-    in_vmem = pl.BlockSpec(memory_space=pltpu.VMEM)
-
+def call(kernel, *shapes, space=pltpu.VMEM, scratch=(), limit=32 * 1024 * 1024):
     def run(*args):
         return pl.pallas_call(
             kernel,
             out_shape=[jax.ShapeDtypeStruct(shape, F32) for shape in shapes],
-            in_specs=[in_vmem] * len(args),
-            out_specs=[in_vmem] * len(shapes),
-            compiler_params=pltpu.CompilerParams(vmem_limit_bytes=32 * 1024 * 1024),
+            in_specs=[pl.BlockSpec(memory_space=space)] * len(args),
+            out_specs=[pl.BlockSpec(memory_space=pltpu.VMEM)] * len(shapes),
+            scratch_shapes=scratch,
+            compiler_params=pltpu.CompilerParams(vmem_limit_bytes=limit),
         )(*args)
 
     return run
@@ -196,16 +208,19 @@
 
 def per_device(recharge, conductivity, storage):
     size = {axis: lax.axis_size(axis) for axis in ALL}
-    own, out = call(pack_layer, (12, 32, 256), (7, 32, 256))(recharge, conductivity, storage)
+    block = (4, 32, 256)
+    scratch = [pltpu.VMEM(block, F32)] * 3 + [pltpu.SemaphoreType.DMA((3,))]
+    near = size["x"] * size["c"]
+    own, out, side = call(
+        pack_own, (12, 32, 256), (7, 32, 256), (near, 32, 128), space=pltpu.HBM, scratch=scratch
+    )(*(pltpu.with_memory_space_constraint(v, pltpu.HBM) for v in (recharge, conductivity, storage)))
     beside = lax.ppermute(out, "c", [(0, 1), (1, 0)])
-    low, high = call(pack_north, (32, 128), (32, 128))(own, beside)
-    up, down = chain(size["x"])
-    from_low, from_high = lax.ppermute(high, "x", up), lax.ppermute(low, "x", down)
-    wide, low, high = call(pack_east, (SLABS, 32, 384), (6, 8, 384), (6, 8, 384))(own, beside, from_low, from_high)
+    side = lax.all_to_all(side, ("x", "c"), 0, 0)
+    pack = functools.partial(pack_east, size["x"])
+    wide, low, high = call(pack, (SLABS, 32, 384), (6, 8, 384), (6, 8, 384))(own, beside, side)
     up, down = chain(size["z"] * size["y"])
     from_low, from_high = lax.ppermute(high, EAST, up), lax.ppermute(low, EAST, down)
     first = size["y"] * size["x"]
-    block = (4, 32, 256)
     z, q, w, u, sums = call(operate, block, block, block, block, (first, 1, 128))(wide, from_low, from_high)
     sums = lax.all_to_all(sums, ("y", "x"), 0, 0)
     sums = spread_sum(jnp.sum(sums, axis=0), ("z", "c"), size["z"] * size["c"])

time: 73.4 us -> 69.9 us (0.952)
  blocking collectives: 41.7 us -> 46.9 us
  waiting for transfers between devices: 8.07 us -> 3.8 us
  local copies, waits for them, and re-layouts: 2.72 us -> 0.01 us
  starting transfers between devices: 17.6 us -> 15 us
  Pallas kernels: 2.16 us -> 3.2 us
    all_to_all x0 -> x1, blocking collectives: none -> 7.67 us  [per_device(): side = lax.all_to_all(side, ('x', 'c'), 0, 0)]
    ppermute x2 -> x0, waiting for transfers between devices: 3.18 us -> none  [the longest x1 3.17 us: per_device(): lax.ppermute(low, 'x', down)]
    unnamed x6 -> x0, local copies, waits for them, and re-layouts: 2.7 us -> none
    ppermute x2 -> x0, starting transfers between devices: 2.58 us -> none  [the longest x1 1.29 us: per_device(): lax.ppermute(low, 'x', down)]
    all_to_all x1, blocking collectives: 29.1 us -> 27.7 us  [spread_sum(): lax.all_to_all(jnp.broadcast_to(line[None], (count, 1, 128)), axes, 0, 0)]
    all_to_all x1, blocking collectives: 12.7 us -> 11.6 us  [per_device(): sums = lax.all_to_all(sums, ('y', 'x'), 0, 0)]
    ppermute x1, waiting for transfers between devices: 1.09 us -> 0.01 us  [per_device(): beside = lax.ppermute(out, 'c', [(0, 1), (1, 0)])]
    pallas_call x5 -> x4, Pallas kernels: 2.16 us -> 3.2 us  [run(): pl.pallas_call(kernel, out_shape=[jax.ShapeDtypeStruct(shape, F32) for sh...]
  transfers between devices with their start and end apart: 5 -> 3, of which waited for: 4 -> 2; matrix products, arithmetic and copies ran while one was open for 0% -> 0% of each run, Pallas kernels for 0% -> 0%
where the time goes in v2:
time: 69.9 us; the launch traced here: 69.6 us
  blocking collectives  46.9 us (67%)
  starting transfers between devices  15 us (21%)
  waiting for transfers between devices  3.8 us (5%)
  Pallas kernels  3.2 us (5%)
    all_to_all x1, blocking collectives, spread_sum(): lax.all_to_all(jnp.broadcast_to(line[None], (count, 1, 128)), axes, 0, 0)  27.7 us
    ppermute x1, starting transfers between devices, per_device(): beside = lax.ppermute(out, 'c', [(0, 1), (1, 0)])  12.4 us
    all_to_all x1, blocking collectives, per_device(): sums = lax.all_to_all(sums, ('y', 'x'), 0, 0)  11.6 us
    all_to_all x1, blocking collectives, per_device(): side = lax.all_to_all(side, ('x', 'c'), 0, 0)  7.67 us
    ppermute x1, waiting for transfers between devices, per_device(): lax.ppermute(low, EAST, down)  3.71 us
    pallas_call x4, Pallas kernels, run(): pl.pallas_call(kernel, out_shape=[jax.ShapeDtypeStruct(shape, F32) for sh...  3.2 us
  transfers between devices with their start and end apart: 3, of which 2 were waited for; matrix products, arithmetic and copies ran while one was open for 0% of the time, Pallas kernels for 0%

profile of v2, /device:TPU:1, one launch (start us, length us, event | category | flops | bytes accessed | tf_op | source)
XLA Modules:
  0.0 69.6 jit_solution(9285476769086071434)
XLA Ops:
  0.6 1.2 %shard_map.50 = (f32[12,32,256]{2,1,0:T(8,128)S(1)}, f32[7,32,256]{2,1,0:T(8,128)S(1)}, f32[8,32,128]{2,1,0:T(8,128)S(1)}) custom-call(f32[4,32,256]{2,1,0:T(8,128)} %r_hbm.1, f32[4,32,256]{2,1,0:T(8,128)} %k_hbm.1, f32[4,32,256]{2,1,0:T(8,128)} %s_hbm.1), custom_call_target="tpu_custom_call" | custom-call | tf_op jit(solution)/shard_map/pallas_call | solution.py:188
  1.9 12.4 %collective-permute-start = (f32[7,32,256]{2,1,0:T(8,128)S(1)}, f32[7,32,256]{2,1,0:T(8,128)S(1)}, u32[]{:S(2)}, u32[]{:S(2)}) collective-permute-start(f32[7,32,256]{2,1,0:T(8,128)S(1)} %get-tuple-element.14), channel_id=1, source_target_pairs={{0,1},{1,0},{2,3},{3,2},{4,5},{5,4},{6,7},{7,6},{8,9},{9,8},{10,11... | collective-permute-start | bytes 688136 | tf_op jit(solution)/shard_map/ppermute | solution.py:217
  14.3 7.7 %all_to_all.15.side_ref = f32[8,32,128]{2,1,0:T(8,128)S(1)} all-to-all(f32[8,32,128]{2,1,0:T(8,128)S(1)} %get-tuple-element.15), channel_id=1, replica_groups=mesh['z'=12,'y'=8,'x'=4,'c'=2] {'x','c'}, dimensions={0} | all-to-all | bytes 262144 | tf_op jit(solution)/shard_map/all_to_all | solution.py:218
  22.0 0.0 collective-permute-done.in_ref
  22.0 0.2 shard_map.51
  22.2 1.3 %collective-permute-start.1 = (f32[6,8,384]{2,1,0:T(8,128)S(1)}, f32[6,8,384]{2,1,0:T(8,128)S(1)}, u32[]{:S(2)}, u32[]{:S(2)}) collective-permute-start(f32[6,8,384]{2,1,0:T(8,128)S(1)} %get-tuple-element.17), channel_id=1, source_target_pairs={{0,8},{8,16},{16,24},{24,32},{32,40},{40,48},{48,56},{56,64},{64,7... | collective-permute-start | bytes 221192 | tf_op jit(solution)/shard_map/ppermute | solution.py:222
  23.5 1.3 %collective-permute-start.2 = (f32[6,8,384]{2,1,0:T(8,128)S(1)}, f32[6,8,384]{2,1,0:T(8,128)S(1)}, u32[]{:S(2)}, u32[]{:S(2)}) collective-permute-start(f32[6,8,384]{2,1,0:T(8,128)S(1)} %get-tuple-element.18), channel_id=1, source_target_pairs={{8,0},{16,8},{24,16},{32,24},{40,32},{48,40},{56,48},{64,56},{72,6... | collective-permute-start | bytes 221192 | tf_op jit(solution)/shard_map/ppermute | solution.py:222
  24.8 0.1 collective-permute-done.1.from_low_ref
  24.9 3.7 %collective-permute-done.2.from_high_ref = f32[6,8,384]{2,1,0:T(8,128)S(1)} collective-permute-done((f32[6,8,384]{2,1,0:T(8,128)S(1)}, f32[6,8,384]{2,1,0:T(8,128)S(1)}, u32[]{:S(2)}, u32[]{:S(2)}) %collective-permute-start.2) | collective-permute-done | bytes 73760 | tf_op jit(solution)/shard_map/ppermute | solution.py:222
  28.6 0.9 %shard_map.52 = (f32[4,32,256]{2,1,0:T(8,128)S(1)}, f32[4,32,256]{2,1,0:T(8,128)S(1)}, f32[4,32,256]{2,1,0:T(8,128)S(1)}, f32[4,32,256]{2,1,0:T(8,128)S(1)}, f32[32,1,128]{2,1,0:T(1,128)S(1)}) custom-call(f32[19,32,384]{2,1,0:T(8,128)S(1)} %get-tuple-element.16.wide_ref, f32[6,8,384]{2,1,0:T(8,128)S(1)} %collective-permute-done.1.from_low_ref, ...), custom_call_target="tpu_custom_call" | custom-call | tf_op jit(solution)/shard_map/pallas_call | solution.py:188
  29.5 11.6 %all_to_all.16 = f32[32,1,128]{2,1,0:T(1,128)S(1)} all-to-all(f32[32,1,128]{2,1,0:T(1,128)S(1)} %get-tuple-element.19), channel_id=1, replica_groups=mesh['z'=12,'y'=8,'x'=4,'c'=2] {'y','x'}, dimensions={0} | all-to-all | bytes 32768 | tf_op jit(solution)/shard_map/all_to_all | solution.py:225
  41.1 0.1 reduce_sum.9
  41.1 27.7 %all_to_all.17.sums_ref = f32[24,1,128]{2,1,0:T(1,128)S(1)} all-to-all(f32[24,1,128]{2,1,0:T(1,128)S(1)} %broadcast_in_dim.2), channel_id=1, replica_groups=mesh['z'=12,'y'=8,'x'=4,'c'=2] {'z','c'}, dimensions={0} | all-to-all | bytes 24576 | tf_op jit(solution)/shard_map/all_to_all | solution.py:206
  68.8 0.8 %shard_map.53 = (f32[4,32,256]{2,1,0:T(8,128)}, f32[4,32,256]{2,1,0:T(8,128)}) custom-call(f32[24,1,128]{2,1,0:T(1,128)S(1)} %all_to_all.17.sums_ref, f32[12,32,256]{2,1,0:T(8,128)S(1)} %get-tuple-element.13.own_ref.r_ref, f32[4,32,256]{2,1,0:T(8,128)S(1)} %get-tuple-element.20.z_ref, f32[4,32,256]{2,1,0:T(8,128)S(1)} %get-tuple-element.21.q_ref, ...), custom_call_target="tpu_custom_call" | custom-call | tf_op jit(solution)/shard_map/pallas_call | solution.py:188
  (1 shorter events, 0.0 us)
Async XLA Ops:
  1.9 20.1 %collective-permute-start = (f32[7,32,256]{2,1,0:T(8,128)S(1)}, f32[7,32,256]{2,1,0:T(8,128)S(1)}, u32[]{:S(2)}, u32[]{:S(2)}) collective-permute-start(f32[7,32,256]{2,1,0:T(8,128)S(1)} %get-tuple-element.14), channel_id=1, source_target_pairs={{0,1},{1,0},{2,3},{3,2},{4,5},{5,4},{6,7},{7,6},{8,9},{9,8},{10,11... | collective-permute-start | bytes 688136 | tf_op jit(solution)/shard_map/ppermute | solution.py:217
  22.2 2.7 %collective-permute-start.1 = (f32[6,8,384]{2,1,0:T(8,128)S(1)}, f32[6,8,384]{2,1,0:T(8,128)S(1)}, u32[]{:S(2)}, u32[]{:S(2)}) collective-permute-start(f32[6,8,384]{2,1,0:T(8,128)S(1)} %get-tuple-element.17), channel_id=1, source_target_pairs={{0,8},{8,16},{16,24},{24,32},{32,40},{40,48},{48,56},{56,64},{64,7... | collective-permute-start | bytes 221192 | tf_op jit(solution)/shard_map/ppermute | solution.py:222
  23.5 5.1 %collective-permute-start.2 = (f32[6,8,384]{2,1,0:T(8,128)S(1)}, f32[6,8,384]{2,1,0:T(8,128)S(1)}, u32[]{:S(2)}, u32[]{:S(2)}) collective-permute-start(f32[6,8,384]{2,1,0:T(8,128)S(1)} %get-tuple-element.18), channel_id=1, source_target_pairs={{8,0},{16,8},{24,16},{32,24},{40,32},{48,40},{56,48},{64,56},{72,6... | collective-permute-start | bytes 221192 | tf_op jit(solution)/shard_map/ppermute | solution.py:222

commit v3 on v2

--- a/solution.py
+++ b/solution.py
@@ -1,7 +1,9 @@
 import functools
+import math
 
 import jax
 import jax.numpy as jnp
+import numpy as np
 from jax import lax
 from jax.experimental import pallas as pl
 from jax.experimental.pallas import tpu as pltpu
@@ -202,8 +204,13 @@
     return up, [(target, source) for source, target in up]
 
 
-def spread_sum(line, axes, count):
-    return lax.all_to_all(jnp.broadcast_to(line[None], (count, 1, 128)), axes, 0, 0)
+def groups(size, axes):
+    ids = np.arange(math.prod(size.values())).reshape([size[axis] for axis in ALL])
+    for i, first in enumerate((3 * size["z"] // 4, size["y"] // 2, size["x"] // 2, size["c"] // 2)):
+        ids = np.roll(ids, -first, i)
+    own = [ALL.index(axis) for axis in axes]
+    rest = [i for i in range(len(ALL)) if i not in own]
+    return ids.transpose(rest + own).reshape(-1, math.prod(size[axis] for axis in axes)).tolist()
 
 
 def per_device(recharge, conductivity, storage):
@@ -220,10 +227,11 @@
     wide, low, high = call(pack, (SLABS, 32, 384), (6, 8, 384), (6, 8, 384))(own, beside, side)
     up, down = chain(size["z"] * size["y"])
     from_low, from_high = lax.ppermute(high, EAST, up), lax.ppermute(low, EAST, down)
-    first = size["y"] * size["x"]
-    z, q, w, u, sums = call(operate, block, block, block, block, (first, 1, 128))(wide, from_low, from_high)
-    sums = lax.all_to_all(sums, ("y", "x"), 0, 0)
-    sums = spread_sum(jnp.sum(sums, axis=0), ("z", "c"), size["z"] * size["c"])
+    z, q, w, u, sums = call(operate, block, block, block, block, (size["z"] * size["c"], 1, 128))(wide, from_low, from_high)
+    sums = lax.all_to_all(sums, ALL, 0, 0, axis_index_groups=groups(size, ("z", "c")))
+    line = jnp.sum(sums, axis=0)
+    sums = jnp.broadcast_to(line[None], (size["y"] * size["x"], 1, 128))
+    sums = lax.all_to_all(sums, ALL, 0, 0, axis_index_groups=groups(size, ("y", "x")))
     return tuple(call(finish, block, block)(sums, own, z, q, w, u))
 
 

time: 69.9 us -> 63 us (0.901)
  blocking collectives: 46.9 us -> 39.3 us
    all_to_all x2, blocking collectives: 39.2 us -> 31.7 us  [the longest x1 18.6 us: per_device(): lax.all_to_all(sums, ALL, 0, 0, axis_index_groups=groups(size, ('z', 'c')))]
where the time goes in v3:
time: 63 us; the launch traced here: 62.1 us
  blocking collectives  39.3 us (62%)
  starting transfers between devices  15 us (24%)
  waiting for transfers between devices  3.8 us (6%)
  Pallas kernels  3.21 us (5%)
  between operations  0.68 us (1%)
    all_to_all x1, blocking collectives, per_device(): lax.all_to_all(sums, ALL, 0, 0, axis_index_groups=groups(size, ('z', 'c')))  18.6 us
    all_to_all x1, blocking collectives, per_device(): lax.all_to_all(sums, ALL, 0, 0, axis_index_groups=groups(size, ('y', 'x')))  13.1 us
    ppermute x1, starting transfers between devices, per_device(): beside = lax.ppermute(out, 'c', [(0, 1), (1, 0)])  12.4 us
    all_to_all x1, blocking collectives, per_device(): side = lax.all_to_all(side, ('x', 'c'), 0, 0)  7.67 us
    ppermute x1, waiting for transfers between devices, per_device(): lax.ppermute(low, EAST, down)  3.71 us
    pallas_call x4, Pallas kernels, run(): pl.pallas_call(kernel, out_shape=[jax.ShapeDtypeStruct(shape, F32) for sh...  3.21 us
    ppermute x1, starting transfers between devices, per_device(): lax.ppermute(high, EAST, up)  1.29 us
    ppermute x1, starting transfers between devices, per_device(): lax.ppermute(low, EAST, down)  1.29 us
  transfers between devices with their start and end apart: 3, of which 2 were waited for; matrix products, arithmetic and copies ran while one was open for 0% of the time, Pallas kernels for 0%

profile of v3, /device:TPU:1, one launch (start us, length us, event | category | flops | bytes accessed | tf_op | source)
XLA Modules:
  0.0 62.1 jit_solution(5260587252389132444)
XLA Ops:
  0.6 1.2 %shard_map.50 = (f32[12,32,256]{2,1,0:T(8,128)S(1)}, f32[7,32,256]{2,1,0:T(8,128)S(1)}, f32[8,32,128]{2,1,0:T(8,128)S(1)}) custom-call(f32[4,32,256]{2,1,0:T(8,128)} %r_hbm.1, f32[4,32,256]{2,1,0:T(8,128)} %k_hbm.1, f32[4,32,256]{2,1,0:T(8,128)} %s_hbm.1), custom_call_target="tpu_custom_call" | custom-call | tf_op jit(solution)/shard_map/pallas_call | solution.py:190
  1.9 12.4 %collective-permute-start = (f32[7,32,256]{2,1,0:T(8,128)S(1)}, f32[7,32,256]{2,1,0:T(8,128)S(1)}, u32[]{:S(2)}, u32[]{:S(2)}) collective-permute-start(f32[7,32,256]{2,1,0:T(8,128)S(1)} %get-tuple-element.14), channel_id=1, source_target_pairs={{0,1},{1,0},{2,3},{3,2},{4,5},{5,4},{6,7},{7,6},{8,9},{9,8},{10,11... | collective-permute-start | bytes 688136 | tf_op jit(solution)/shard_map/ppermute | solution.py:224
  14.3 7.7 %all_to_all.15.side_ref = f32[8,32,128]{2,1,0:T(8,128)S(1)} all-to-all(f32[8,32,128]{2,1,0:T(8,128)S(1)} %get-tuple-element.15), channel_id=1, replica_groups=mesh['z'=12,'y'=8,'x'=4,'c'=2] {'x','c'}, dimensions={0} | all-to-all | bytes 262144 | tf_op jit(solution)/shard_map/all_to_all | solution.py:225
  22.0 0.0 collective-permute-done.in_ref
  22.0 0.2 shard_map.51
  22.2 1.3 %collective-permute-start.1 = (f32[6,8,384]{2,1,0:T(8,128)S(1)}, f32[6,8,384]{2,1,0:T(8,128)S(1)}, u32[]{:S(2)}, u32[]{:S(2)}) collective-permute-start(f32[6,8,384]{2,1,0:T(8,128)S(1)} %get-tuple-element.17), channel_id=1, source_target_pairs={{0,8},{8,16},{16,24},{24,32},{32,40},{40,48},{48,56},{56,64},{64,7... | collective-permute-start | bytes 221192 | tf_op jit(solution)/shard_map/ppermute | solution.py:229
  23.5 1.3 %collective-permute-start.2 = (f32[6,8,384]{2,1,0:T(8,128)S(1)}, f32[6,8,384]{2,1,0:T(8,128)S(1)}, u32[]{:S(2)}, u32[]{:S(2)}) collective-permute-start(f32[6,8,384]{2,1,0:T(8,128)S(1)} %get-tuple-element.18), channel_id=1, source_target_pairs={{8,0},{16,8},{24,16},{32,24},{40,32},{48,40},{56,48},{64,56},{72,6... | collective-permute-start | bytes 221192 | tf_op jit(solution)/shard_map/ppermute | solution.py:229
  24.8 0.1 collective-permute-done.1.from_low_ref
  24.9 3.7 %collective-permute-done.2.from_high_ref = f32[6,8,384]{2,1,0:T(8,128)S(1)} collective-permute-done((f32[6,8,384]{2,1,0:T(8,128)S(1)}, f32[6,8,384]{2,1,0:T(8,128)S(1)}, u32[]{:S(2)}, u32[]{:S(2)}) %collective-permute-start.2) | collective-permute-done | bytes 73760 | tf_op jit(solution)/shard_map/ppermute | solution.py:229
  28.6 0.9 %shard_map.52 = (f32[4,32,256]{2,1,0:T(8,128)S(1)}, f32[4,32,256]{2,1,0:T(8,128)S(1)}, f32[4,32,256]{2,1,0:T(8,128)S(1)}, f32[4,32,256]{2,1,0:T(8,128)S(1)}, f32[24,1,128]{2,1,0:T(1,128)S(1)}) custom-call(f32[19,32,384]{2,1,0:T(8,128)S(1)} %get-tuple-element.16.wide_ref, f32[6,8,384]{2,1,0:T(8,128)S(1)} %collective-permute-done.1.from_low_ref, ...), custom_call_target="tpu_custom_call" | custom-call | tf_op jit(solution)/shard_map/pallas_call | solution.py:190
  29.5 18.6 %all_to_all.16 = f32[24,1,128]{2,1,0:T(1,128)S(1)} all-to-all(f32[24,1,128]{2,1,0:T(1,128)S(1)} %get-tuple-element.19), channel_id=1, replica_groups={{613,612,677,676,741,740,37,36,101,100,165,164,229,228,293,292,357,356,..., dimensions={0} | all-to-all | bytes 24576 | tf_op jit(solution)/shard_map/all_to_all | solution.py:231
  48.2 13.1 %all_to_all.17.sums_ref = f32[32,1,128]{2,1,0:T(1,128)S(1)} all-to-all(f32[32,1,128]{2,1,0:T(1,128)S(1)} %broadcast_in_dim.2), channel_id=1, replica_groups={{613,615,609,611,621,623,617,619,629,631,625,627,637,639,633,635,581,58..., dimensions={0} | all-to-all | bytes 32768 | tf_op jit(solution)/shard_map/all_to_all | solution.py:234
  61.2 0.8 %shard_map.53 = (f32[4,32,256]{2,1,0:T(8,128)}, f32[4,32,256]{2,1,0:T(8,128)}) custom-call(f32[32,1,128]{2,1,0:T(1,128)S(1)} %all_to_all.17.sums_ref, f32[12,32,256]{2,1,0:T(8,128)S(1)} %get-tuple-element.13.own_ref.r_ref, f32[4,32,256]{2,1,0:T(8,128)S(1)} %get-tuple-element.20.z_ref, f32[4,32,256]{2,1,0:T(8,128)S(1)} %get-tuple-element.21.q_ref, ...), custom_call_target="tpu_custom_call" | custom-call | tf_op jit(solution)/shard_map/pallas_call | solution.py:190
  (2 shorter events, 0.1 us)
Async XLA Ops:
  1.9 20.1 %collective-permute-start = (f32[7,32,256]{2,1,0:T(8,128)S(1)}, f32[7,32,256]{2,1,0:T(8,128)S(1)}, u32[]{:S(2)}, u32[]{:S(2)}) collective-permute-start(f32[7,32,256]{2,1,0:T(8,128)S(1)} %get-tuple-element.14), channel_id=1, source_target_pairs={{0,1},{1,0},{2,3},{3,2},{4,5},{5,4},{6,7},{7,6},{8,9},{9,8},{10,11... | collective-permute-start | bytes 688136 | tf_op jit(solution)/shard_map/ppermute | solution.py:224
  22.2 2.7 %collective-permute-start.1 = (f32[6,8,384]{2,1,0:T(8,128)S(1)}, f32[6,8,384]{2,1,0:T(8,128)S(1)}, u32[]{:S(2)}, u32[]{:S(2)}) collective-permute-start(f32[6,8,384]{2,1,0:T(8,128)S(1)} %get-tuple-element.17), channel_id=1, source_target_pairs={{0,8},{8,16},{16,24},{24,32},{32,40},{40,48},{48,56},{56,64},{64,7... | collective-permute-start | bytes 221192 | tf_op jit(solution)/shard_map/ppermute | solution.py:229
  23.5 5.1 %collective-permute-start.2 = (f32[6,8,384]{2,1,0:T(8,128)S(1)}, f32[6,8,384]{2,1,0:T(8,128)S(1)}, u32[]{:S(2)}, u32[]{:S(2)}) collective-permute-start(f32[6,8,384]{2,1,0:T(8,128)S(1)} %get-tuple-element.18), channel_id=1, source_target_pairs={{8,0},{16,8},{24,16},{32,24},{40,32},{48,40},{56,48},{64,56},{72,6... | collective-permute-start | bytes 221192 | tf_op jit(solution)/shard_map/ppermute | solution.py:229

commit v4 on v3

--- a/solution.py
+++ b/solution.py
@@ -14,99 +14,90 @@
 F32 = jnp.float32
 
 NK, NR = 7, 6
-SLABS = NK + 2 * NR
 SIDE = [("k", j) for j in range(6)] + [("r", j) for j in range(5)] + [("s", j) for j in range(5)]
 OWN = {"k": 0, "r": 4, "s": 8}
 HALF = 64
 
 
-def slab_index(name, j):
-    return {"k": 0, "r": NK, "s": NK + NR}[name] + j
-
-
-def pack_own(r_hbm, k_hbm, s_hbm, own_ref, out_ref, side_ref, r_ref, k_ref, s_ref, arrived):
+def sends_low_first():
+    return lax.rem(lax.axis_index("y"), 2) == 0
+
+
+def pack_own(r_hbm, k_hbm, s_hbm, own_ref, first_ref, second_ref, r_ref, k_ref, s_ref, arrived):
     copies = [
         pltpu.make_async_copy(source, target, arrived.at[i])
         for i, (source, target) in enumerate(((k_hbm, k_ref), (r_hbm, r_ref), (s_hbm, s_ref)))
     ]
     for copy in copies:
         copy.start()
-    core = lax.axis_index("c")
-    lane = lax.broadcasted_iota(jnp.int32, (32, 128), 1)
-    line = jnp.zeros((32, 128), F32)
-    at = 0
-    for copy, ref, name, count in zip(copies, (k_ref, r_ref, s_ref), "krs", (3, 2, 2)):
+    core, flip = lax.axis_index("c"), sends_low_first()
+    row = lax.broadcasted_iota(jnp.int32, (8, 256), 0)
+    for copy, ref, name in zip(copies, (k_ref, r_ref, s_ref), "krs"):
         copy.wait()
         for j in range(4):
-            slab = ref[jnp.where(core == 0, j, 3 - j)]
+            own_ref[OWN[name] + j] = ref[jnp.where(core == 0, j, 3 - j)]
+    for j in range(4):
+        k, r, s = (own_ref[OWN[name] + j] for name in "krs")
+        low = jnp.where(row < 3, k[:8], jnp.where(row < 5, pltpu.roll(r[:8], 3, 0), pltpu.roll(s[:8], 5, 0)))
+        high = jnp.where(row >= 5, k[24:], jnp.where(row >= 3, pltpu.roll(r[24:], 5, 0), pltpu.roll(s[24:], 3, 0)))
+        first_ref[j] = jnp.where(flip, low, high)
+        second_ref[j] = jnp.where(flip, high, low)
+
+
+def widen(own_ref, first_ref, second_ref, tall_ref, out_ref, side_ref):
+    flip = sends_low_first()
+    row = lax.broadcasted_iota(jnp.int32, (8, 256), 0)
+    lane = lax.broadcasted_iota(jnp.int32, (40, 128), 1)
+    line = jnp.zeros((40, 128), F32)
+    at = 0
+    for name, count in (("k", 3), ("r", 2), ("s", 2)):
+        slabs = []
+        for j in range(4):
+            below = jnp.where(flip, first_ref[j], second_ref[j])
+            above = jnp.where(flip, second_ref[j], first_ref[j])
+            if name == "k":
+                beyond = jnp.where(row < 3, above, jnp.where(row >= 5, below, 0.0))
+            else:
+                up, down = (5, 3) if name == "r" else (3, 5)
+                beyond = jnp.where(row < 2, pltpu.roll(above, up, 0), jnp.where(row >= 6, pltpu.roll(below, down, 0), 0.0))
             i = OWN[name] + j
-            own_ref[i] = slab
+            slab = jnp.concatenate([own_ref[i], beyond], axis=0)
+            tall_ref[i] = slab
+            slabs.append(slab)
             low, high = slab[:, :128], pltpu.roll(slab[:, 128:], 3 * i + HALF + 3, 1)
             low = pltpu.roll(low, 3 * i, 1) if i else low
             line = jnp.where((lane >= 3 * i) & (lane < 3 * i + 3), low, line)
             line = jnp.where((lane >= HALF + 3 * i) & (lane < HALF + 3 * i + 3), high, line)
         for j in range(count):
-            out_ref[at] = ref[jnp.where(core == 0, 3 - j, j)]
+            out_ref[at] = slabs[3 - j]
             at += 1
     for i in range(side_ref.shape[0]):
         side_ref[i] = line
 
 
-def main_slab(own_ref, in_ref, name, j):
-    beside = {"k": 0, "r": 3, "s": 5}[name]
-    return own_ref[OWN[name] + j] if j < 4 else in_ref[beside + j - 4]
-
-
-def pack_east(north_count, own_ref, in_ref, side_ref, wide_ref, low_ref, high_ref):
-    lane = lax.broadcasted_iota(jnp.int32, (32, 128), 1)
+def harmonic(first, second):
+    return 2.0 * first * second / jnp.maximum(first + second, 1e-30)
+
+
+def operate(north_count, tall_ref, in_ref, side_ref, z_ref, q_ref, w_ref, u_ref, sums_ref):
+    lane = lax.broadcasted_iota(jnp.int32, (40, 128), 1)
     core, place = lax.axis_index("c"), lax.axis_index("x")
     up, down = jnp.minimum(place + 1, north_count - 1), jnp.maximum(place - 1, 0)
     has_up, has_down = place < north_count - 1, place > 0
     same = (side_ref[2 * up + core], side_ref[2 * down + core])
     other = (side_ref[2 * up + 1 - core], side_ref[2 * down + 1 - core])
     take_up, take_down = (lane < 3) & has_up, (lane >= 125) & has_down
-    for name, count in (("k", NK), ("r", NR), ("s", NR)):
-        for j in range(count):
-            at = slab_index(name, j)
-            wide_ref[at, :, :256] = main_slab(own_ref, in_ref, name, j)
-            beyond = jnp.zeros((32, 128), F32)
-            if (name, j) in SIDE:
-                above, below = same if j < 4 else other
-                i = OWN[name] + (j if j < 4 else 7 - j)
-                above = pltpu.roll(above, 128 - 3 * i, 1) if i else above
-                below = pltpu.roll(below, (125 - HALF - 3 * i) % 128, 1)
-                beyond = jnp.where(take_up, above, jnp.where(take_down, below, 0.0))
-            wide_ref[at, :, 256:] = beyond
-    row = lax.broadcasted_iota(jnp.int32, (8, 384), 0)
-    for j in range(6):
-        low, high = wide_ref[j, 0:8, :], wide_ref[j, 24:32, :]
-        if j < 5:
-            r, s = slab_index("r", j), slab_index("s", j)
-            low = jnp.where(row < 3, low, jnp.where(row < 5, pltpu.roll(wide_ref[r, 0:8, :], 3, 0), pltpu.roll(wide_ref[s, 0:8, :], 5, 0)))
-            high = jnp.where(row >= 5, high, jnp.where(row >= 3, pltpu.roll(wide_ref[r, 24:32, :], 5, 0), pltpu.roll(wide_ref[s, 24:32, :], 3, 0)))
-        low_ref[j] = low
-        high_ref[j] = high
-
-
-def harmonic(first, second):
-    return 2.0 * first * second / jnp.maximum(first + second, 1e-30)
-
-
-def operate(wide_ref, from_low_ref, from_high_ref, z_ref, q_ref, w_ref, u_ref, sums_ref):
-    row = lax.broadcasted_iota(jnp.int32, (8, 384), 0)
 
     def whole(name, j):
-        main = wide_ref[slab_index(name, j)]
-        if (name, j) not in SIDE:
-            beyond = jnp.zeros((8, 384), F32)
-        else:
-            above, below = from_high_ref[j], from_low_ref[j]
-            if name == "k":
-                beyond = jnp.where(row < 3, above, jnp.where(row >= 5, below, 0.0))
-            else:
-                up, down = (5, 3) if name == "r" else (3, 5)
-                beyond = jnp.where(row < 2, pltpu.roll(above, up, 0), jnp.where(row >= 6, pltpu.roll(below, down, 0), 0.0))
-        return jnp.concatenate([main, beyond], axis=0)
+        main = tall_ref[OWN[name] + j] if j < 4 else in_ref[{"k": 0, "r": 3, "s": 5}[name] + j - 4]
+        beyond = jnp.zeros((40, 128), F32)
+        if (name, j) in SIDE:
+            above, below = same if j < 4 else other
+            i = OWN[name] + (j if j < 4 else 7 - j)
+            above = pltpu.roll(above, 128 - 3 * i, 1) if i else above
+            below = pltpu.roll(below, (125 - HALF - 3 * i) % 128, 1)
+            beyond = jnp.where(take_up, above, jnp.where(take_down, below, 0.0))
+        return jnp.concatenate([main, beyond], axis=1)
 
     def north(v):
         return pltpu.roll(v, 383, 1)
@@ -152,7 +143,7 @@
         for ref, v in zip((z_ref, q_ref, w_ref, u_ref), own):
             ref[j] = v
         zo, qo, wo, uo = own
-        rz = wide_ref[slab_index("r", j), :, :256] * zo
+        rz = tall_ref[OWN["r"] + j, :32, :] * zo
         for i, product in enumerate((rz, zo * qo, qo * wo, wo * uo)):
             for a in range(4):
                 for b in range(2):
@@ -199,9 +190,9 @@
     return run
 
 
-def chain(count):
-    up = [(i, i + 1) for i in range(count - 1)]
-    return up, [(target, source) for source, target in up]
+def pairs(count, start):
+    up = [(i, i + 1) for i in range(start, count - 1, 2)]
+    return up + [(target, source) for source, target in up]
 
 
 def groups(size, axes):
@@ -218,16 +209,16 @@
     block = (4, 32, 256)
     scratch = [pltpu.VMEM(block, F32)] * 3 + [pltpu.SemaphoreType.DMA((3,))]
     near = size["x"] * size["c"]
-    own, out, side = call(
-        pack_own, (12, 32, 256), (7, 32, 256), (near, 32, 128), space=pltpu.HBM, scratch=scratch
+    own, first, second = call(
+        pack_own, (12, 32, 256), (4, 8, 256), (4, 8, 256), space=pltpu.HBM, scratch=scratch
     )(*(pltpu.with_memory_space_constraint(v, pltpu.HBM) for v in (recharge, conductivity, storage)))
+    odd, even = pairs(size["z"] * size["y"], 1), pairs(size["z"] * size["y"], 0)
+    first, second = lax.ppermute(first, EAST, odd), lax.ppermute(second, EAST, even)
+    tall, out, side = call(widen, (12, 40, 256), (7, 40, 256), (near, 40, 128))(own, first, second)
     beside = lax.ppermute(out, "c", [(0, 1), (1, 0)])
     side = lax.all_to_all(side, ("x", "c"), 0, 0)
-    pack = functools.partial(pack_east, size["x"])
-    wide, low, high = call(pack, (SLABS, 32, 384), (6, 8, 384), (6, 8, 384))(own, beside, side)
-    up, down = chain(size["z"] * size["y"])
-    from_low, from_high = lax.ppermute(high, EAST, up), lax.ppermute(low, EAST, down)
-    z, q, w, u, sums = call(operate, block, block, block, block, (size["z"] * size["c"], 1, 128))(wide, from_low, from_high)
+    apply_both = functools.partial(operate, size["x"])
+    z, q, w, u, sums = call(apply_both, block, block, block, block, (size["z"] * size["c"], 1, 128))(tall, beside, side)
     sums = lax.all_to_all(sums, ALL, 0, 0, axis_index_groups=groups(size, ("z", "c")))
     line = jnp.sum(sums, axis=0)
     sums = jnp.broadcast_to(line[None], (size["y"] * size["x"], 1, 128))

time: 63 us -> 62 us (0.984)
  starting transfers between devices: 15 us -> 17.6 us
  waiting for transfers between devices: 3.8 us -> 1.28 us
  blocking collectives: 39.3 us -> 38.3 us
    ppermute x2, starting transfers between devices: 2.59 us -> 7.24 us  [the longest x1 6.58 us: per_device(): lax.ppermute(second, EAST, even)]
    all_to_all x1, blocking collectives: 13.1 us -> 10.5 us  [per_device(): lax.all_to_all(sums, ALL, 0, 0, axis_index_groups=groups(size, ('y', 'x')))]
    ppermute x2, waiting for transfers between devices: 3.8 us -> 1.28 us  [the longest x1 1.28 us: per_device(): lax.ppermute(second, EAST, even)]
    ppermute x1, starting transfers between devices: 12.4 us -> 10.4 us  [per_device(): beside = lax.ppermute(out, 'c', [(0, 1), (1, 0)])]
    all_to_all x1, blocking collectives: 18.6 us -> 19.8 us  [per_device(): lax.all_to_all(sums, ALL, 0, 0, axis_index_groups=groups(size, ('z', 'c')))]
  transfers between devices with their start and end apart: 3 -> 3, of which waited for: 2 -> 1; matrix products, arithmetic and copies ran while one was open for 0% -> 0% of each run, Pallas kernels for 0% -> 0%
where the time goes in v4:
time: 62 us; the launch traced here: 61 us
  blocking collectives  38.3 us (62%)
  starting transfers between devices  17.6 us (28%)
  Pallas kernels  3.14 us (5%)
  waiting for transfers between devices  1.28 us (2%)
  between operations  0.69 us (1%)
    all_to_all x1, blocking collectives, per_device(): lax.all_to_all(sums, ALL, 0, 0, axis_index_groups=groups(size, ('z', 'c')))  19.8 us
    all_to_all x1, blocking collectives, per_device(): lax.all_to_all(sums, ALL, 0, 0, axis_index_groups=groups(size, ('y', 'x')))  10.5 us
    ppermute x1, starting transfers between devices, per_device(): beside = lax.ppermute(out, 'c', [(0, 1), (1, 0)])  10.4 us
    all_to_all x1, blocking collectives, per_device(): side = lax.all_to_all(side, ('x', 'c'), 0, 0)  7.98 us
    ppermute x1, starting transfers between devices, per_device(): lax.ppermute(second, EAST, even)  6.58 us
    pallas_call x4, Pallas kernels, run(): pl.pallas_call(kernel, out_shape=[jax.ShapeDtypeStruct(shape, F32) for sh...  3.14 us
    ppermute x1, waiting for transfers between devices, per_device(): lax.ppermute(second, EAST, even)  1.28 us
  transfers between devices with their start and end apart: 3, of which 1 were waited for; matrix products, arithmetic and copies ran while one was open for 0% of the time, Pallas kernels for 0%

profile of v4, /device:TPU:1, one launch (start us, length us, event | category | flops | bytes accessed | tf_op | source)
XLA Modules:
  0.0 61.0 jit_solution(5351421874883946032)
XLA Ops:
  0.6 1.1 %shard_map.50 = (f32[12,32,256]{2,1,0:T(8,128)S(1)}, f32[4,8,256]{2,1,0:T(8,128)S(1)}, f32[4,8,256]{2,1,0:T(8,128)S(1)}) custom-call(f32[4,32,256]{2,1,0:T(8,128)} %r_hbm.1, f32[4,32,256]{2,1,0:T(8,128)} %k_hbm.1, f32[4,32,256]{2,1,0:T(8,128)} %s_hbm.1), custom_call_target="tpu_custom_call" | custom-call | tf_op jit(solution)/shard_map/pallas_call | solution.py:181
  1.7 0.7 %collective-permute-start = (f32[4,8,256]{2,1,0:T(8,128)S(1)}, f32[4,8,256]{2,1,0:T(8,128)S(1)}, u32[]{:S(2)}, u32[]{:S(2)}) collective-permute-start(f32[4,8,256]{2,1,0:T(8,128)S(1)} %get-tuple-element.14), channel_id=1, source_target_pairs={{8,16},{24,32},{40,48},{56,64},{72,80},{88,96},{104,112},{120,128}... | collective-permute-start | bytes 98312 | tf_op jit(solution)/shard_map/ppermute | solution.py:216
  2.4 6.6 %collective-permute-start.1 = (f32[4,8,256]{2,1,0:T(8,128)S(1)}, f32[4,8,256]{2,1,0:T(8,128)S(1)}, u32[]{:S(2)}, u32[]{:S(2)}) collective-permute-start(f32[4,8,256]{2,1,0:T(8,128)S(1)} %get-tuple-element.15), channel_id=1, source_target_pairs={{0,8},{16,24},{32,40},{48,56},{64,72},{80,88},{96,104},{112,120},{... | collective-permute-start | bytes 98312 | tf_op jit(solution)/shard_map/ppermute | solution.py:216
  9.0 0.0 collective-permute-done.first_ref
  9.0 1.3 %collective-permute-done.1.second_ref = f32[4,8,256]{2,1,0:T(8,128)S(1)} collective-permute-done((f32[4,8,256]{2,1,0:T(8,128)S(1)}, f32[4,8,256]{2,1,0:T(8,128)S(1)}, u32[]{:S(2)}, u32[]{:S(2)}) %collective-permute-start.1) | collective-permute-done | bytes 32800 | tf_op jit(solution)/shard_map/ppermute | solution.py:216
  10.3 0.2 shard_map.51
  10.5 10.4 %collective-permute-start.2 = (f32[7,40,256]{2,1,0:T(8,128)S(1)}, f32[7,40,256]{2,1,0:T(8,128)S(1)}, u32[]{:S(2)}, u32[]{:S(2)}) collective-permute-start(f32[7,40,256]{2,1,0:T(8,128)S(1)} %get-tuple-element.17), channel_id=1, source_target_pairs={{0,1},{1,0},{2,3},{3,2},{4,5},{5,4},{6,7},{7,6},{8,9},{9,8},{10,11... | collective-permute-start | bytes 860168 | tf_op jit(solution)/shard_map/ppermute | solution.py:218
  20.8 8.0 %all_to_all.15.side_ref = f32[8,40,128]{2,1,0:T(8,128)S(1)} all-to-all(f32[8,40,128]{2,1,0:T(8,128)S(1)} %get-tuple-element.18), channel_id=1, replica_groups=mesh['z'=12,'y'=8,'x'=4,'c'=2] {'x','c'}, dimensions={0} | all-to-all | bytes 327680 | tf_op jit(solution)/shard_map/all_to_all | solution.py:219
  28.8 0.0 collective-permute-done.2.in_ref
  28.8 1.0 %shard_map.52 = (f32[4,32,256]{2,1,0:T(8,128)S(1)}, f32[4,32,256]{2,1,0:T(8,128)S(1)}, f32[4,32,256]{2,1,0:T(8,128)S(1)}, f32[4,32,256]{2,1,0:T(8,128)S(1)}, f32[24,1,128]{2,1,0:T(1,128)S(1)}) custom-call(f32[12,40,256]{2,1,0:T(8,128)S(1)} %get-tuple-element.16.tall_ref, f32[7,40,256]{2,1,0:T(8,128)S(1)} %collective-permute-done.2.in_ref, ...), custom_call_target="tpu_custom_call" | custom-call | tf_op jit(solution)/shard_map/pallas_call | solution.py:181
  29.8 19.8 %all_to_all.16 = f32[24,1,128]{2,1,0:T(1,128)S(1)} all-to-all(f32[24,1,128]{2,1,0:T(1,128)S(1)} %get-tuple-element.19), channel_id=1, replica_groups={{613,612,677,676,741,740,37,36,101,100,165,164,229,228,293,292,357,356,..., dimensions={0} | all-to-all | bytes 24576 | tf_op jit(solution)/shard_map/all_to_all | solution.py:222
  49.7 10.5 %all_to_all.17.sums_ref = f32[32,1,128]{2,1,0:T(1,128)S(1)} all-to-all(f32[32,1,128]{2,1,0:T(1,128)S(1)} %broadcast_in_dim.2), channel_id=1, replica_groups={{613,615,609,611,621,623,617,619,629,631,625,627,637,639,633,635,581,58..., dimensions={0} | all-to-all | bytes 32768 | tf_op jit(solution)/shard_map/all_to_all | solution.py:225
  60.2 0.8 %shard_map.53 = (f32[4,32,256]{2,1,0:T(8,128)}, f32[4,32,256]{2,1,0:T(8,128)}) custom-call(f32[32,1,128]{2,1,0:T(1,128)S(1)} %all_to_all.17.sums_ref, f32[12,32,256]{2,1,0:T(8,128)S(1)} %get-tuple-element.13.own_ref.r_ref, f32[4,32,256]{2,1,0:T(8,128)S(1)} %get-tuple-element.20.z_ref, f32[4,32,256]{2,1,0:T(8,128)S(1)} %get-tuple-element.21.q_ref, ...), custom_call_target="tpu_custom_call" | custom-call | tf_op jit(solution)/shard_map/pallas_call | solution.py:181
  (2 shorter events, 0.1 us)
Async XLA Ops:
  1.7 7.3 %collective-permute-start = (f32[4,8,256]{2,1,0:T(8,128)S(1)}, f32[4,8,256]{2,1,0:T(8,128)S(1)}, u32[]{:S(2)}, u32[]{:S(2)}) collective-permute-start(f32[4,8,256]{2,1,0:T(8,128)S(1)} %get-tuple-element.14), channel_id=1, source_target_pairs={{8,16},{24,32},{40,48},{56,64},{72,80},{88,96},{104,112},{120,128}... | collective-permute-start | bytes 98312 | tf_op jit(solution)/shard_map/ppermute | solution.py:216
  2.4 7.9 %collective-permute-start.1 = (f32[4,8,256]{2,1,0:T(8,128)S(1)}, f32[4,8,256]{2,1,0:T(8,128)S(1)}, u32[]{:S(2)}, u32[]{:S(2)}) collective-permute-start(f32[4,8,256]{2,1,0:T(8,128)S(1)} %get-tuple-element.15), channel_id=1, source_target_pairs={{0,8},{16,24},{32,40},{48,56},{64,72},{80,88},{96,104},{112,120},{... | collective-permute-start | bytes 98312 | tf_op jit(solution)/shard_map/ppermute | solution.py:216
  10.5 18.4 %collective-permute-start.2 = (f32[7,40,256]{2,1,0:T(8,128)S(1)}, f32[7,40,256]{2,1,0:T(8,128)S(1)}, u32[]{:S(2)}, u32[]{:S(2)}) collective-permute-start(f32[7,40,256]{2,1,0:T(8,128)S(1)} %get-tuple-element.17), channel_id=1, source_target_pairs={{0,1},{1,0},{2,3},{3,2},{4,5},{5,4},{6,7},{7,6},{8,9},{9,8},{10,11... | collective-permute-start | bytes 860168 | tf_op jit(solution)/shard_map/ppermute | solution.py:218

commit v5 on v4

--- a/solution.py
+++ b/solution.py
@@ -16,7 +16,12 @@
 NK, NR = 7, 6
 SIDE = [("k", j) for j in range(6)] + [("r", j) for j in range(5)] + [("s", j) for j in range(5)]
 OWN = {"k": 0, "r": 4, "s": 8}
-HALF = 64
+WIDTH = {"k": 3, "r": 2, "s": 2}
+HALF = 32
+
+
+def first_lane(name, j):
+    return {"k": 0, "r": 12, "s": 20}[name] + WIDTH[name] * j
 
 
 def sends_low_first():
@@ -44,14 +49,21 @@
         second_ref[j] = jnp.where(flip, high, low)
 
 
-def widen(own_ref, first_ref, second_ref, tall_ref, out_ref, side_ref):
+def pack_layer(own_ref, out_ref):
+    at = 0
+    for name, count in (("k", 3), ("r", 2), ("s", 2)):
+        for j in range(count):
+            out_ref[at] = own_ref[OWN[name] + 3 - j]
+            at += 1
+
+
+def widen(own_ref, first_ref, second_ref, tall_ref, side_ref):
     flip = sends_low_first()
     row = lax.broadcasted_iota(jnp.int32, (8, 256), 0)
     lane = lax.broadcasted_iota(jnp.int32, (40, 128), 1)
     line = jnp.zeros((40, 128), F32)
-    at = 0
-    for name, count in (("k", 3), ("r", 2), ("s", 2)):
-        slabs = []
+    rows = {}
+    for name in "krs":
         for j in range(4):
             below = jnp.where(flip, first_ref[j], second_ref[j])
             above = jnp.where(flip, second_ref[j], first_ref[j])
@@ -60,19 +72,29 @@
             else:
                 up, down = (5, 3) if name == "r" else (3, 5)
                 beyond = jnp.where(row < 2, pltpu.roll(above, up, 0), jnp.where(row >= 6, pltpu.roll(below, down, 0), 0.0))
+            rows[name, j] = beyond
             i = OWN[name] + j
             slab = jnp.concatenate([own_ref[i], beyond], axis=0)
             tall_ref[i] = slab
-            slabs.append(slab)
-            low, high = slab[:, :128], pltpu.roll(slab[:, 128:], 3 * i + HALF + 3, 1)
-            low = pltpu.roll(low, 3 * i, 1) if i else low
-            line = jnp.where((lane >= 3 * i) & (lane < 3 * i + 3), low, line)
-            line = jnp.where((lane >= HALF + 3 * i) & (lane < HALF + 3 * i + 3), high, line)
-        for j in range(count):
-            out_ref[at] = slabs[3 - j]
-            at += 1
+            at, width = first_lane(name, j), WIDTH[name]
+            low, high = slab[:, :128], pltpu.roll(slab[:, 128:], at + HALF + width, 1)
+            low = pltpu.roll(low, at, 1) if at else low
+            line = jnp.where((lane >= at) & (lane < at + width), low, line)
+            line = jnp.where((lane >= HALF + at) & (lane < HALF + at + width), high, line)
+    folded = jnp.concatenate([pltpu.roll(line[24:], 64, 1), jnp.zeros((8, 128), F32)], axis=0)
+    line = jnp.where(lane[:24] < 64, line[:24], folded)
     for i in range(side_ref.shape[0]):
         side_ref[i] = line
+    mixed = rows["k", 3]
+    for to, back, slab in ((2, 5, rows["k", 2]), (3, 4, rows["r", 3])):
+        mixed = jnp.where(row == to, pltpu.roll(slab, to, 0), mixed)
+        mixed = jnp.where(row == back, pltpu.roll(slab, back + 1, 0), mixed)
+    last, narrow = rows["s", 3], row[:, :128]
+    right = jnp.where(narrow == 1, pltpu.roll(last[:, 128:], 1, 0), pltpu.roll(last[:, 128:], 7, 0))
+    last = jnp.where((narrow == 0) | (narrow == 7), last[:, :128], right)
+    to = 2 * lax.axis_index("x") + 1 - lax.axis_index("c")
+    for i, tile in enumerate((mixed[:, :128], mixed[:, 128:], last)):
+        side_ref[to, 8 * i : 8 * i + 8, :] = tile
 
 
 def harmonic(first, second):
@@ -84,18 +106,42 @@
     core, place = lax.axis_index("c"), lax.axis_index("x")
     up, down = jnp.minimum(place + 1, north_count - 1), jnp.maximum(place - 1, 0)
     has_up, has_down = place < north_count - 1, place > 0
-    same = (side_ref[2 * up + core], side_ref[2 * down + core])
-    other = (side_ref[2 * up + 1 - core], side_ref[2 * down + 1 - core])
-    take_up, take_down = (lane < 3) & has_up, (lane >= 125) & has_down
+
+    def line(at):
+        folded = side_ref[at]
+        return jnp.concatenate([folded, pltpu.roll(folded[:16], 64, 1)], axis=0)
+
+    same = (line(2 * up + core), line(2 * down + core))
+    other = (line(2 * up + 1 - core), line(2 * down + 1 - core))
+
+    row = lax.broadcasted_iota(jnp.int32, (8, 256), 0)
+    across = side_ref[2 * place + 1 - core]
+    mixed, last, narrow = jnp.concatenate([across[:8], across[8:16]], axis=1), across[16:], row[:, :128]
+    right = jnp.where(narrow == 0, pltpu.roll(last, 7, 0), pltpu.roll(last, 1, 0))
+    spread = {
+        ("k", 4): (mixed, mixed),
+        ("k", 5): (pltpu.roll(mixed, 6, 0), pltpu.roll(mixed, 2, 0)),
+        ("r", 4): (pltpu.roll(mixed, 5, 0), pltpu.roll(mixed, 3, 0)),
+        ("s", 4): (jnp.concatenate([last, right], axis=1),) * 2,
+    }
 
     def whole(name, j):
-        main = tall_ref[OWN[name] + j] if j < 4 else in_ref[{"k": 0, "r": 3, "s": 5}[name] + j - 4]
+        if j < 4:
+            main = tall_ref[OWN[name] + j]
+        else:
+            tile = jnp.zeros((8, 256), F32)
+            if (name, j) in spread:
+                deep = 2 if (name, j) == ("k", 4) else 1
+                above, below = spread[name, j]
+                tile = jnp.where(row < deep, above, jnp.where(row >= 8 - deep, below, 0.0))
+            main = jnp.concatenate([in_ref[{"k": 0, "r": 3, "s": 5}[name] + j - 4], tile], axis=0)
         beyond = jnp.zeros((40, 128), F32)
         if (name, j) in SIDE:
             above, below = same if j < 4 else other
-            i = OWN[name] + (j if j < 4 else 7 - j)
-            above = pltpu.roll(above, 128 - 3 * i, 1) if i else above
-            below = pltpu.roll(below, (125 - HALF - 3 * i) % 128, 1)
+            at, width = first_lane(name, j if j < 4 else 7 - j), WIDTH[name]
+            above = pltpu.roll(above, 128 - at, 1) if at else above
+            below = pltpu.roll(below, 128 - HALF - width - at, 1)
+            take_up, take_down = (lane < width) & has_up, (lane >= 128 - width) & has_down
             beyond = jnp.where(take_up, above, jnp.where(take_down, below, 0.0))
         return jnp.concatenate([main, beyond], axis=1)
 
@@ -214,8 +260,9 @@
     )(*(pltpu.with_memory_space_constraint(v, pltpu.HBM) for v in (recharge, conductivity, storage)))
     odd, even = pairs(size["z"] * size["y"], 1), pairs(size["z"] * size["y"], 0)
     first, second = lax.ppermute(first, EAST, odd), lax.ppermute(second, EAST, even)
-    tall, out, side = call(widen, (12, 40, 256), (7, 40, 256), (near, 40, 128))(own, first, second)
+    (out,) = call(pack_layer, (7, 32, 256))(own)
     beside = lax.ppermute(out, "c", [(0, 1), (1, 0)])
+    tall, side = call(widen, (12, 40, 256), (near, 24, 128))(own, first, second)
     side = lax.all_to_all(side, ("x", "c"), 0, 0)
     apply_both = functools.partial(operate, size["x"])
     z, q, w, u, sums = call(apply_both, block, block, block, block, (size["z"] * size["c"], 1, 128))(tall, beside, side)

time: 62 us -> 61.2 us (0.987)
  starting transfers between devices: 17.6 us -> 15 us
  waiting for transfers between devices: 1.28 us -> 2.73 us
    ppermute x1, starting transfers between devices: 6.58 us -> 1.92 us  [per_device(): lax.ppermute(second, EAST, even)]
    ppermute x1, starting transfers between devices: 10.4 us -> 12.4 us  [per_device(): beside = lax.ppermute(out, 'c', [(0, 1), (1, 0)])]
    ppermute x1, waiting for transfers between devices: 1.28 us -> 2.72 us  [per_device(): lax.ppermute(second, EAST, even)]
    pallas_call x4 -> x5, Pallas kernels: 3.14 us -> 3.17 us  [run(): pl.pallas_call(kernel, out_shape=[jax.ShapeDtypeStruct(shape, F32) for sh...]
where the time goes in v5:
time: 61.2 us; the launch traced here: 60.3 us
  blocking collectives  38.6 us (63%)
  starting transfers between devices  15 us (25%)
  Pallas kernels  3.17 us (5%)
  waiting for transfers between devices  2.73 us (4%)
  between operations  0.69 us (1%)
    all_to_all x1, blocking collectives, per_device(): lax.all_to_all(sums, ALL, 0, 0, axis_index_groups=groups(size, ('z', 'c')))  19.6 us
    ppermute x1, starting transfers between devices, per_device(): beside = lax.ppermute(out, 'c', [(0, 1), (1, 0)])  12.4 us
    all_to_all x1, blocking collectives, per_device(): lax.all_to_all(sums, ALL, 0, 0, axis_index_groups=groups(size, ('y', 'x')))  10.5 us
    all_to_all x1, blocking collectives, per_device(): side = lax.all_to_all(side, ('x', 'c'), 0, 0)  8.51 us
    pallas_call x5, Pallas kernels, run(): pl.pallas_call(kernel, out_shape=[jax.ShapeDtypeStruct(shape, F32) for sh...  3.17 us
    ppermute x1, waiting for transfers between devices, per_device(): lax.ppermute(second, EAST, even)  2.72 us
    ppermute x1, starting transfers between devices, per_device(): lax.ppermute(second, EAST, even)  1.92 us
  transfers between devices with their start and end apart: 3, of which 1 were waited for; matrix products, arithmetic and copies ran while one was open for 0% of the time, Pallas kernels for 0%

profile of v5, /device:TPU:1, one launch (start us, length us, event | category | flops | bytes accessed | tf_op | source)
XLA Modules:
  0.0 60.3 jit_solution(15307909347146898688)
XLA Ops:
  0.6 1.1 %shard_map.50 = (f32[12,32,256]{2,1,0:T(8,128)S(1)}, f32[4,8,256]{2,1,0:T(8,128)S(1)}, f32[4,8,256]{2,1,0:T(8,128)S(1)}) custom-call(f32[4,32,256]{2,1,0:T(8,128)} %r_hbm.1, f32[4,32,256]{2,1,0:T(8,128)} %k_hbm.1, f32[4,32,256]{2,1,0:T(8,128)} %s_hbm.1), custom_call_target="tpu_custom_call" | custom-call | tf_op jit(solution)/shard_map/pallas_call | solution.py:227
  1.7 12.4 %collective-permute-start.2 = (f32[7,32,256]{2,1,0:T(8,128)S(1)}, f32[7,32,256]{2,1,0:T(8,128)S(1)}, u32[]{:S(2)}, u32[]{:S(2)}) collective-permute-start(f32[7,32,256]{2,1,0:T(8,128)S(1)} %shard_map.52), channel_id=1, source_target_pairs={{0,1},{1,0},{2,3},{3,2},{4,5},{5,4},{6,7},{7,6},{8,9},{9,8},{10,11... | collective-permute-start | bytes 688136 | tf_op jit(solution)/shard_map/ppermute | solution.py:264
  14.2 0.7 %collective-permute-start = (f32[4,8,256]{2,1,0:T(8,128)S(1)}, f32[4,8,256]{2,1,0:T(8,128)S(1)}, u32[]{:S(2)}, u32[]{:S(2)}) collective-permute-start(f32[4,8,256]{2,1,0:T(8,128)S(1)} %get-tuple-element.13), channel_id=1, source_target_pairs={{8,16},{24,32},{40,48},{56,64},{72,80},{88,96},{104,112},{120,128}... | collective-permute-start | bytes 98312 | tf_op jit(solution)/shard_map/ppermute | solution.py:262
  14.8 1.9 %collective-permute-start.1 = (f32[4,8,256]{2,1,0:T(8,128)S(1)}, f32[4,8,256]{2,1,0:T(8,128)S(1)}, u32[]{:S(2)}, u32[]{:S(2)}) collective-permute-start(f32[4,8,256]{2,1,0:T(8,128)S(1)} %get-tuple-element.14), channel_id=1, source_target_pairs={{0,8},{16,24},{32,40},{48,56},{64,72},{80,88},{96,104},{112,120},{... | collective-permute-start | bytes 98312 | tf_op jit(solution)/shard_map/ppermute | solution.py:262
  16.8 0.0 collective-permute-done.first_ref
  16.8 2.7 %collective-permute-done.1.second_ref = f32[4,8,256]{2,1,0:T(8,128)S(1)} collective-permute-done((f32[4,8,256]{2,1,0:T(8,128)S(1)}, f32[4,8,256]{2,1,0:T(8,128)S(1)}, u32[]{:S(2)}, u32[]{:S(2)}) %collective-permute-start.1) | collective-permute-done | bytes 32800 | tf_op jit(solution)/shard_map/ppermute | solution.py:262
  19.5 0.2 shard_map.51
  19.7 8.5 %all_to_all.15.side_ref = f32[8,24,128]{2,1,0:T(8,128)S(1)} all-to-all(f32[8,24,128]{2,1,0:T(8,128)S(1)} %get-tuple-element.16), channel_id=1, replica_groups=mesh['z'=12,'y'=8,'x'=4,'c'=2] {'x','c'}, dimensions={0} | all-to-all | bytes 196608 | tf_op jit(solution)/shard_map/all_to_all | solution.py:266
  28.2 0.0 collective-permute-done.2.in_ref
  28.2 1.0 %shard_map.53 = (f32[4,32,256]{2,1,0:T(8,128)S(1)}, f32[4,32,256]{2,1,0:T(8,128)S(1)}, f32[4,32,256]{2,1,0:T(8,128)S(1)}, f32[4,32,256]{2,1,0:T(8,128)S(1)}, f32[24,1,128]{2,1,0:T(1,128)S(1)}) custom-call(f32[12,40,256]{2,1,0:T(8,128)S(1)} %get-tuple-element.15.tall_ref, f32[7,32,256]{2,1,0:T(8,128)S(1)} %collective-permute-done.2.in_ref, ...), custom_call_target="tpu_custom_call" | custom-call | tf_op jit(solution)/shard_map/pallas_call | solution.py:227
  29.3 19.6 %all_to_all.16 = f32[24,1,128]{2,1,0:T(1,128)S(1)} all-to-all(f32[24,1,128]{2,1,0:T(1,128)S(1)} %get-tuple-element.17), channel_id=1, replica_groups={{613,612,677,676,741,740,37,36,101,100,165,164,229,228,293,292,357,356,..., dimensions={0} | all-to-all | bytes 24576 | tf_op jit(solution)/shard_map/all_to_all | solution.py:269
  48.9 10.5 %all_to_all.17.sums_ref = f32[32,1,128]{2,1,0:T(1,128)S(1)} all-to-all(f32[32,1,128]{2,1,0:T(1,128)S(1)} %broadcast_in_dim.2), channel_id=1, replica_groups={{613,615,609,611,621,623,617,619,629,631,625,627,637,639,633,635,581,58..., dimensions={0} | all-to-all | bytes 32768 | tf_op jit(solution)/shard_map/all_to_all | solution.py:272
  59.4 0.8 %shard_map.54 = (f32[4,32,256]{2,1,0:T(8,128)}, f32[4,32,256]{2,1,0:T(8,128)}) custom-call(f32[32,1,128]{2,1,0:T(1,128)S(1)} %all_to_all.17.sums_ref, f32[12,32,256]{2,1,0:T(8,128)S(1)} %get-tuple-element.12.own_ref.r_ref, f32[4,32,256]{2,1,0:T(8,128)S(1)} %get-tuple-element.18.z_ref, f32[4,32,256]{2,1,0:T(8,128)S(1)} %get-tuple-element.19.q_ref, ...), custom_call_target="tpu_custom_call" | custom-call | tf_op jit(solution)/shard_map/pallas_call | solution.py:227
  (3 shorter events, 0.1 us)
Async XLA Ops:
  1.7 26.5 %collective-permute-start.2 = (f32[7,32,256]{2,1,0:T(8,128)S(1)}, f32[7,32,256]{2,1,0:T(8,128)S(1)}, u32[]{:S(2)}, u32[]{:S(2)}) collective-permute-start(f32[7,32,256]{2,1,0:T(8,128)S(1)} %shard_map.52), channel_id=1, source_target_pairs={{0,1},{1,0},{2,3},{3,2},{4,5},{5,4},{6,7},{7,6},{8,9},{9,8},{10,11... | collective-permute-start | bytes 688136 | tf_op jit(solution)/shard_map/ppermute | solution.py:264
  14.2 2.6 %collective-permute-start = (f32[4,8,256]{2,1,0:T(8,128)S(1)}, f32[4,8,256]{2,1,0:T(8,128)S(1)}, u32[]{:S(2)}, u32[]{:S(2)}) collective-permute-start(f32[4,8,256]{2,1,0:T(8,128)S(1)} %get-tuple-element.13), channel_id=1, source_target_pairs={{8,16},{24,32},{40,48},{56,64},{72,80},{88,96},{104,112},{120,128}... | collective-permute-start | bytes 98312 | tf_op jit(solution)/shard_map/ppermute | solution.py:262
  14.8 4.7 %collective-permute-start.1 = (f32[4,8,256]{2,1,0:T(8,128)S(1)}, f32[4,8,256]{2,1,0:T(8,128)S(1)}, u32[]{:S(2)}, u32[]{:S(2)}) collective-permute-start(f32[4,8,256]{2,1,0:T(8,128)S(1)} %get-tuple-element.14), channel_id=1, source_target_pairs={{0,8},{16,24},{32,40},{48,56},{64,72},{80,88},{96,104},{112,120},{... | collective-permute-start | bytes 98312 | tf_op jit(solution)/shard_map/ppermute | solution.py:262

commit v6 on v5

--- a/solution.py
+++ b/solution.py
@@ -92,7 +92,7 @@
     last, narrow = rows["s", 3], row[:, :128]
     right = jnp.where(narrow == 1, pltpu.roll(last[:, 128:], 1, 0), pltpu.roll(last[:, 128:], 7, 0))
     last = jnp.where((narrow == 0) | (narrow == 7), last[:, :128], right)
-    to = 2 * lax.axis_index("x") + 1 - lax.axis_index("c")
+    to = near_place(lax.axis_index("x"), side_ref.shape[0] // 2) + lax.axis_index("c")
     for i, tile in enumerate((mixed[:, :128], mixed[:, 128:], last)):
         side_ref[to, 8 * i : 8 * i + 8, :] = tile
 
@@ -105,17 +105,18 @@
     lane = lax.broadcasted_iota(jnp.int32, (40, 128), 1)
     core, place = lax.axis_index("c"), lax.axis_index("x")
     up, down = jnp.minimum(place + 1, north_count - 1), jnp.maximum(place - 1, 0)
+    up, down = near_place(up, north_count), near_place(down, north_count)
     has_up, has_down = place < north_count - 1, place > 0
 
     def line(at):
         folded = side_ref[at]
         return jnp.concatenate([folded, pltpu.roll(folded[:16], 64, 1)], axis=0)
 
-    same = (line(2 * up + core), line(2 * down + core))
-    other = (line(2 * up + 1 - core), line(2 * down + 1 - core))
+    same = (line(up + 1 - core), line(down + 1 - core))
+    other = (line(up + core), line(down + core))
 
     row = lax.broadcasted_iota(jnp.int32, (8, 256), 0)
-    across = side_ref[2 * place + 1 - core]
+    across = side_ref[near_place(place, north_count) + core]
     mixed, last, narrow = jnp.concatenate([across[:8], across[8:16]], axis=1), across[16:], row[:, :128]
     right = jnp.where(narrow == 0, pltpu.roll(last, 7, 0), pltpu.roll(last, 1, 0))
     spread = {
@@ -250,6 +251,15 @@
     return ids.transpose(rest + own).reshape(-1, math.prod(size[axis] for axis in axes)).tolist()
 
 
+def near_groups(size):
+    ids = np.arange(math.prod(size.values())).reshape(-1, size["x"], size["c"])
+    return np.roll(ids, -(size["x"] // 2), 1)[:, :, ::-1].reshape(-1, size["x"] * size["c"]).tolist()
+
+
+def near_place(place, count):
+    return 2 * lax.rem(place + count - count // 2, count)
+
+
 def per_device(recharge, conductivity, storage):
     size = {axis: lax.axis_size(axis) for axis in ALL}
     block = (4, 32, 256)
@@ -263,7 +273,7 @@
     (out,) = call(pack_layer, (7, 32, 256))(own)
     beside = lax.ppermute(out, "c", [(0, 1), (1, 0)])
     tall, side = call(widen, (12, 40, 256), (near, 24, 128))(own, first, second)
-    side = lax.all_to_all(side, ("x", "c"), 0, 0)
+    side = lax.all_to_all(side, ALL, 0, 0, axis_index_groups=near_groups(size))
     apply_both = functools.partial(operate, size["x"])
     z, q, w, u, sums = call(apply_both, block, block, block, block, (size["z"] * size["c"], 1, 128))(tall, beside, side)
     sums = lax.all_to_all(sums, ALL, 0, 0, axis_index_groups=groups(size, ("z", "c")))

time: 61.2 us -> 59.4 us (0.971)
  blocking collectives: 38.6 us -> 36.8 us
    all_to_all x1, blocking collectives: 19.6 us -> 18.2 us  [per_device(): lax.all_to_all(sums, ALL, 0, 0, axis_index_groups=groups(size, ('z', 'c')))]
    all_to_all x1, blocking collectives: 8.51 us -> 7.74 us  [per_device(): side = lax.all_to_all(side, ALL, 0, 0, axis_index_groups=near_groups(size))]
where the time goes in v6:
time: 59.4 us; the launch traced here: 58.5 us
  blocking collectives  36.8 us (62%)
  starting transfers between devices  15 us (25%)
  Pallas kernels  3.17 us (5%)
  waiting for transfers between devices  2.73 us (5%)
  between operations  0.69 us (1%)
    all_to_all x1, blocking collectives, per_device(): lax.all_to_all(sums, ALL, 0, 0, axis_index_groups=groups(size, ('z', 'c')))  18.2 us
    ppermute x1, starting transfers between devices, per_device(): beside = lax.ppermute(out, 'c', [(0, 1), (1, 0)])  12.4 us
    all_to_all x1, blocking collectives, per_device(): lax.all_to_all(sums, ALL, 0, 0, axis_index_groups=groups(size, ('y', 'x')))  10.9 us
    all_to_all x1, blocking collectives, per_device(): side = lax.all_to_all(side, ALL, 0, 0, axis_index_groups=near_groups(size))  7.74 us
    pallas_call x5, Pallas kernels, run(): pl.pallas_call(kernel, out_shape=[jax.ShapeDtypeStruct(shape, F32) for sh...  3.17 us
    ppermute x1, waiting for transfers between devices, per_device(): lax.ppermute(second, EAST, even)  2.72 us
    ppermute x1, starting transfers between devices, per_device(): lax.ppermute(second, EAST, even)  1.92 us
  transfers between devices with their start and end apart: 3, of which 1 were waited for; matrix products, arithmetic and copies ran while one was open for 0% of the time, Pallas kernels for 0%

profile of v6, /device:TPU:1, one launch (start us, length us, event | category | flops | bytes accessed | tf_op | source)
XLA Modules:
  0.0 58.5 jit_solution(17406229723560901487)
XLA Ops:
  0.6 1.1 %shard_map.50 = (f32[12,32,256]{2,1,0:T(8,128)S(1)}, f32[4,8,256]{2,1,0:T(8,128)S(1)}, f32[4,8,256]{2,1,0:T(8,128)S(1)}) custom-call(f32[4,32,256]{2,1,0:T(8,128)} %r_hbm.1, f32[4,32,256]{2,1,0:T(8,128)} %k_hbm.1, f32[4,32,256]{2,1,0:T(8,128)} %s_hbm.1), custom_call_target="tpu_custom_call" | custom-call | tf_op jit(solution)/shard_map/pallas_call | solution.py:228
  1.7 12.4 %collective-permute-start.2 = (f32[7,32,256]{2,1,0:T(8,128)S(1)}, f32[7,32,256]{2,1,0:T(8,128)S(1)}, u32[]{:S(2)}, u32[]{:S(2)}) collective-permute-start(f32[7,32,256]{2,1,0:T(8,128)S(1)} %shard_map.52), channel_id=1, source_target_pairs={{0,1},{1,0},{2,3},{3,2},{4,5},{5,4},{6,7},{7,6},{8,9},{9,8},{10,11... | collective-permute-start | bytes 688136 | tf_op jit(solution)/shard_map/ppermute | solution.py:274
  14.2 0.7 %collective-permute-start = (f32[4,8,256]{2,1,0:T(8,128)S(1)}, f32[4,8,256]{2,1,0:T(8,128)S(1)}, u32[]{:S(2)}, u32[]{:S(2)}) collective-permute-start(f32[4,8,256]{2,1,0:T(8,128)S(1)} %get-tuple-element.13), channel_id=1, source_target_pairs={{8,16},{24,32},{40,48},{56,64},{72,80},{88,96},{104,112},{120,128}... | collective-permute-start | bytes 98312 | tf_op jit(solution)/shard_map/ppermute | solution.py:272
  14.8 1.9 %collective-permute-start.1 = (f32[4,8,256]{2,1,0:T(8,128)S(1)}, f32[4,8,256]{2,1,0:T(8,128)S(1)}, u32[]{:S(2)}, u32[]{:S(2)}) collective-permute-start(f32[4,8,256]{2,1,0:T(8,128)S(1)} %get-tuple-element.14), channel_id=1, source_target_pairs={{0,8},{16,24},{32,40},{48,56},{64,72},{80,88},{96,104},{112,120},{... | collective-permute-start | bytes 98312 | tf_op jit(solution)/shard_map/ppermute | solution.py:272
  16.8 0.0 collective-permute-done.first_ref
  16.8 2.7 %collective-permute-done.1.second_ref = f32[4,8,256]{2,1,0:T(8,128)S(1)} collective-permute-done((f32[4,8,256]{2,1,0:T(8,128)S(1)}, f32[4,8,256]{2,1,0:T(8,128)S(1)}, u32[]{:S(2)}, u32[]{:S(2)}) %collective-permute-start.1) | collective-permute-done | bytes 32800 | tf_op jit(solution)/shard_map/ppermute | solution.py:272
  19.5 0.2 shard_map.51
  19.7 7.7 %all_to_all.15.side_ref = f32[8,24,128]{2,1,0:T(8,128)S(1)} all-to-all(f32[8,24,128]{2,1,0:T(8,128)S(1)} %get-tuple-element.16), channel_id=1, replica_groups={{5,4,7,6,1,0,3,2},{13,12,15,14,9,8,11,10},{21,20,23,22,17,16,19,18},{29..., dimensions={0} | all-to-all | bytes 196608 | tf_op jit(solution)/shard_map/all_to_all | solution.py:276
  27.5 0.0 collective-permute-done.2.in_ref
  27.5 1.0 %shard_map.53 = (f32[4,32,256]{2,1,0:T(8,128)S(1)}, f32[4,32,256]{2,1,0:T(8,128)S(1)}, f32[4,32,256]{2,1,0:T(8,128)S(1)}, f32[4,32,256]{2,1,0:T(8,128)S(1)}, f32[24,1,128]{2,1,0:T(1,128)S(1)}) custom-call(f32[12,40,256]{2,1,0:T(8,128)S(1)} %get-tuple-element.15.tall_ref, f32[7,32,256]{2,1,0:T(8,128)S(1)} %collective-permute-done.2.in_ref, ...), custom_call_target="tpu_custom_call" | custom-call | tf_op jit(solution)/shard_map/pallas_call | solution.py:228
  28.5 18.2 %all_to_all.16 = f32[24,1,128]{2,1,0:T(1,128)S(1)} all-to-all(f32[24,1,128]{2,1,0:T(1,128)S(1)} %get-tuple-element.17), channel_id=1, replica_groups={{613,612,677,676,741,740,37,36,101,100,165,164,229,228,293,292,357,356,..., dimensions={0} | all-to-all | bytes 24576 | tf_op jit(solution)/shard_map/all_to_all | solution.py:279
  46.7 10.9 %all_to_all.17.sums_ref = f32[32,1,128]{2,1,0:T(1,128)S(1)} all-to-all(f32[32,1,128]{2,1,0:T(1,128)S(1)} %broadcast_in_dim.2), channel_id=1, replica_groups={{613,615,609,611,621,623,617,619,629,631,625,627,637,639,633,635,581,58..., dimensions={0} | all-to-all | bytes 32768 | tf_op jit(solution)/shard_map/all_to_all | solution.py:282
  57.6 0.8 %shard_map.54 = (f32[4,32,256]{2,1,0:T(8,128)}, f32[4,32,256]{2,1,0:T(8,128)}) custom-call(f32[32,1,128]{2,1,0:T(1,128)S(1)} %all_to_all.17.sums_ref, f32[12,32,256]{2,1,0:T(8,128)S(1)} %get-tuple-element.12.own_ref.r_ref, f32[4,32,256]{2,1,0:T(8,128)S(1)} %get-tuple-element.18.z_ref, f32[4,32,256]{2,1,0:T(8,128)S(1)} %get-tuple-element.19.q_ref, ...), custom_call_target="tpu_custom_call" | custom-call | tf_op jit(solution)/shard_map/pallas_call | solution.py:228
  (3 shorter events, 0.1 us)
Async XLA Ops:
  1.7 25.7 %collective-permute-start.2 = (f32[7,32,256]{2,1,0:T(8,128)S(1)}, f32[7,32,256]{2,1,0:T(8,128)S(1)}, u32[]{:S(2)}, u32[]{:S(2)}) collective-permute-start(f32[7,32,256]{2,1,0:T(8,128)S(1)} %shard_map.52), channel_id=1, source_target_pairs={{0,1},{1,0},{2,3},{3,2},{4,5},{5,4},{6,7},{7,6},{8,9},{9,8},{10,11... | collective-permute-start | bytes 688136 | tf_op jit(solution)/shard_map/ppermute | solution.py:274
  14.2 2.6 %collective-permute-start = (f32[4,8,256]{2,1,0:T(8,128)S(1)}, f32[4,8,256]{2,1,0:T(8,128)S(1)}, u32[]{:S(2)}, u32[]{:S(2)}) collective-permute-start(f32[4,8,256]{2,1,0:T(8,128)S(1)} %get-tuple-element.13), channel_id=1, source_target_pairs={{8,16},{24,32},{40,48},{56,64},{72,80},{88,96},{104,112},{120,128}... | collective-permute-start | bytes 98312 | tf_op jit(solution)/shard_map/ppermute | solution.py:272
  14.8 4.7 %collective-permute-start.1 = (f32[4,8,256]{2,1,0:T(8,128)S(1)}, f32[4,8,256]{2,1,0:T(8,128)S(1)}, u32[]{:S(2)}, u32[]{:S(2)}) collective-permute-start(f32[4,8,256]{2,1,0:T(8,128)S(1)} %get-tuple-element.14), channel_id=1, source_target_pairs={{0,8},{16,24},{32,40},{48,56},{64,72},{80,88},{96,104},{112,120},{... | collective-permute-start | bytes 98312 | tf_op jit(solution)/shard_map/ppermute | solution.py:272
